TPU v7x, 32 devices: a whole 2x2x4 slice. The times are simulated.
32 devices in a mesh: lat: 4 (over z), lon: 2 (over y), tm: 4 (over x, core).
Axes of the slice: x: 2, y: 2, z: 4, core: 2. Of those that a mesh axis runs over, the one named last changes fastest.
Arguments:
- signal: bfloat16 [4, 78, 32, 256], P('tm', None, 'lat', 'lon'), may hold values from -6 to 6
- dictionary: bfloat16 [64, 9984], P('lon'), may hold values from -0.0625 to 0.0625
- codes_init: float32 [4, 64, 8, 64], P('tm', None, 'lat', 'lon'), may hold values from -3 to 3
- thresholds: float32 [64], replicated, may hold values from 0.2 to 2
Outputs:
- codes: float32 [4, 64, 8, 64], P('tm', None, 'lat', 'lon')
- dict_grad: float32 [64, 9984], P('lon')
All inputs are finite; a program needn't handle non-finite values.
Results may differ from a plain program's by a relative error of at most 0.0044.
Values may be sent and summed in bfloat16 or wider, within the bound.
A program may use at most 128 MiB of HBM per device.

v0:
```python
import math

import jax
import jax.numpy as jnp
from jax import lax
from jax.sharding import PartitionSpec as P

ITERS = 2


STEP_SIZE = 0.5


def passed_along(shard, axis, by):
    peers = lax.axis_size(axis)
    pairs = [(i, i + by) for i in range(peers) if 0 <= i + by < peers]
    return lax.ppermute(shard, axis, pairs)


def shifted(block, axis, distance):
    devices = range(lax.axis_size(axis))
    route = [((i - distance) % len(devices), i) for i in devices]
    return lax.ppermute(block, axis, route)


def combos():
    return [(delay, down, right) for delay in (0, 1) for down in (0, 1) for right in (0, 1)]


def to_atoms(local, channels, count):
    shaped = local.reshape(channels, 4, 4, 2, 2, 2, count)
    return shaped.transpose(6, 3, 0, 4, 1, 5, 2).reshape(count, 2 * channels * 64)


def extend_codes(coded):
    atoms, rows, columns = coded.shape
    earlier = passed_along(coded, "tm", 1)
    both = jnp.stack([coded, earlier])
    above = passed_along(both[:, :, -1:, :], "lat", 1)
    both = jnp.concatenate([above, both], axis=2)
    beside = shifted(both[:, :, :, -1:], "lon", 1)
    both = jnp.concatenate([beside, both], axis=3)
    pieces = [
        both[delay, :, 1 - down : 1 - down + rows, 1 - right : 1 - right + columns]
        for delay, down, right in combos()
    ]
    return jnp.stack(pieces).reshape(8 * atoms, rows * columns)


def body(signal, dictionary, codes_init, thresholds):
    channels = signal.shape[1]
    rows = signal.shape[2] // 4
    columns = signal.shape[3] // 4
    patch = channels * 16
    gathered = lax.all_gather(dictionary, "lon", axis=0, tiled=True)
    atoms = gathered.shape[0]
    blocks = (
        gathered.reshape(atoms, 2, channels, 2, 4, 2, 4)
        .transpose(1, 3, 5, 2, 4, 6, 0)
        .reshape(8, patch, atoms)
    )
    synth_matrix = blocks.transpose(1, 0, 2).reshape(patch, 8 * atoms)
    target = (
        signal[0]
        .reshape(channels, rows, 4, columns, 4)
        .transpose(0, 2, 4, 1, 3)
        .reshape(patch, rows * columns)
    )

    def residual_of(current):
        stacked = extend_codes(current.astype(jnp.bfloat16).reshape(atoms, rows, columns))
        synth = jnp.dot(synth_matrix, stacked, preferred_element_type=jnp.float32)
        return ((synth - target).astype(jnp.bfloat16), stacked)

    partial_matrix = blocks.transpose(0, 2, 1).reshape(8 * atoms, patch)
    current = codes_init[0].reshape(atoms, rows * columns)
    moving = current
    momentum_now = 1.0
    shrink = STEP_SIZE * thresholds[:, None]
    for turn in range(ITERS):
        residual, stacked = residual_of(moving)
        terms = jnp.dot(partial_matrix, residual, preferred_element_type=jnp.float32).reshape(
            2, 4, atoms, rows, columns
        )
        later = passed_along(terms[1], "tm", -1)
        joined = (terms[0] + later).reshape(2, 2, atoms, rows, columns)
        below = passed_along(joined[1, :, :, :1, :], "lat", -1)
        moved = jnp.concatenate([joined[1, :, :, 1:, :], below], axis=2)
        summed = joined[0] + moved
        beside = shifted(summed[1, :, :, :1], "lon", -1)
        moved = jnp.concatenate([summed[1, :, :, 1:], beside], axis=2)
        descent = moving - STEP_SIZE * (summed[0] + moved).reshape(atoms, rows * columns)
        updated = jnp.sign(descent) * jnp.maximum(jnp.abs(descent) - shrink, 0.0)
        momentum_next = (1.0 + math.sqrt(1.0 + 4.0 * momentum_now * momentum_now)) / 2.0
        moving = updated + (momentum_now - 1.0) / momentum_next * (updated - current)
        current = updated
        momentum_now = momentum_next
    residual, stacked = residual_of(current)
    positions = lax.axis_size("tm") * lax.axis_size("lat") * lax.axis_size("lon") * rows * columns
    scale = 1.0 / math.sqrt(positions)
    owned_rows = atoms // lax.axis_size("lon")
    local = lax.dot_general(
        residual, stacked, (((1,), (1,)), ((), ())), preferred_element_type=jnp.float32
    )
    total = lax.psum(to_atoms(local, channels, atoms) * scale, ("lat", "lon", "tm"))
    mine = lax.dynamic_slice_in_dim(total, lax.axis_index("lon") * owned_rows, owned_rows, 0)
    return (current.reshape(1, atoms, rows, columns), mine)


def solution(mesh):
    placed = (P("tm", None, "lat", "lon"), P("lon", None), P("tm", None, "lat", "lon"), P())
    return jax.shard_map(
        body,
        mesh=mesh,
        in_specs=placed,
        out_specs=(P("tm", None, "lat", "lon"), P("lon", None)),
        check_vma=False,
    )
```

profile of v0, /device:TPU:0, one launch (start us, length us, event | category | flops | bytes accessed | tf_op | source)
XLA Modules:
  0.0 295.9 jit_solution(817519231102667608)
XLA Ops:
  7.2 0.8 bitcast_convert_fusion
  8.0 2.3 collective-permute-start
  10.3 0.8 constant_dynamic-update-slice_fusion.7
  11.2 4.3 %collective-permute-start.1 = (bf16[2,64,1,32]{1,3,2,0:T(8,128)(2,1)S(1)}, bf16[2,64,1,32]{1,3,2,0:T(8,128)(2,1)S(1)}, u32[]{:S(2)}, u32[]{:S(2)}) collective-permute-start(bf16[2,64,1,32]{1,3,2,0:T(8,128)(2,1)S(1)} %pad_maximum_fusion.10), channel_id=1, source_target_pairs={{0,8},{8,16},{16,24},{1,9},{9,17},{17,25},{2,10},{10,18},{18,26},{... | collective-permute-start | bytes 24584 | tf_op jit(solution)/shard_map/ppermute | solution.py:17
  15.5 1.4 collective-permute-done.1
  16.9 1.6 collective-permute-start.2
  18.6 1.1 copy.53
  19.7 1.4 copy.22
  21.1 0.7 reshape.122
  22.2 23.9 %all-gather.2.cloned.1.call-done = bf16[64,9984]{1,0:T(8,128)(2,1)} async-done(((bf16[32,9984]{1,0:T(8,128)(2,1)}), bf16[64,9984]{1,0:T(8,128)(2,1)}) %all-gather.2.cloned.1.call-update) | async-done | bytes 1277968 | tf_op jit(solution)/shard_map/all_gather | solution.py:55
  46.1 3.8 %copy.18 = bf16[64,9984]{0,1:T(8,128)(2,1)} copy(bf16[64,9984]{1,0:T(8,128)(2,1)} %all-gather.2.cloned.1.call-done) | data formatting | bytes 2555904 | tf_op jit(solution)/shard_map/all_gather | solution.py:55
  49.9 2.6 copy.19
  52.5 2.8 copy.23
  55.3 2.8 copy.20
  58.1 3.1 %fusion.8 = f32[512,64]{0,1:T(8,128)S(1)} fusion(bf16[512,1248]{1,0:T(8,128)(2,1)} %bitcast.176, f32[1248,64]{1,0:T(8,128)S(1)} %reshape.122, bf16[512,64]{0,1:T(8,128)(2,1)S(1)} %reshape.113, bf16[1248,512]{0,1:T(8,128)(2,1)} %bitcast.172), kind=kOutput, calls=%fused_computation.12 | convolution fusion | flops 163737600 | bytes 3072000 | tf_op jit(solution)/shard_map/dot_general | solution.py:82
  61.3 0.7 copy.24
  62.0 1.4 collective-permute-start.3
  63.6 2.1 collective-permute-done.3
  65.7 0.9 copy_add_fusion.1
  66.7 1.3 collective-permute-start.4
  68.0 4.5 %collective-permute-done.4 = f32[2,64,1,32]{1,3,0,2:T(8,128)S(1)} collective-permute-done((f32[2,64,1,32]{1,3,0,2:T(8,128)S(1)}, f32[2,64,1,32]{1,3,0,2:T(8,128)S(1)}, u32[]{:S(2)}, u32[]{:S(2)}) %collective-permute-start.4) | collective-permute-done | bytes 16416 | tf_op jit(solution)/shard_map/ppermute | solution.py:17
  72.5 0.4 collective-permute-start.5
  72.9 3.2 %collective-permute-done.5 = f32[64,2,1]{0,2,1:T(1,128)S(1)} collective-permute-done((f32[64,2,1]{0,2,1:T(1,128)S(1)}, f32[64,2,1]{0,2,1:T(1,128)S(1)}, u32[]{:S(2)}, u32[]{:S(2)}) %collective-permute-start.5) | collective-permute-done | bytes 544 | tf_op jit(solution)/shard_map/ppermute | solution.py:23
  76.2 2.5 collective-permute-start.6
  78.7 0.8 collective-permute-done.6
  79.5 3.4 %collective-permute-start.7 = (bf16[2,64,1,32]{1,3,2,0:T(8,128)(2,1)S(1)}, bf16[2,64,1,32]{1,3,2,0:T(8,128)(2,1)S(1)}, u32[]{:S(2)}, u32[]{:S(2)}) collective-permute-start(bf16[2,64,1,32]{1,3,2,0:T(8,128)(2,1)S(1)} %pad_maximum_fusion.7), channel_id=1, source_target_pairs={{0,8},{8,16},{16,24},{1,9},{9,17},{17,25},{2,10},{10,18},{18,26},{... | collective-permute-start | bytes 24584 | tf_op jit(solution)/shard_map/ppermute | solution.py:17
  82.9 1.4 collective-permute-done.7
  84.3 0.6 collective-permute-start.8
  84.9 3.0 %collective-permute-done.8 = bf16[2,64,3,1]{1,3,2,0:T(2,128)(2,1)S(1)} collective-permute-done((bf16[2,64,3,1]{1,3,2,0:T(2,128)(2,1)S(1)}, bf16[2,64,3,1]{1,3,2,0:T(2,128)(2,1)S(1)}, u32[]{:S(2)}, u32[]{:S(2)}) %collective-permute-start.8) | collective-permute-done | bytes 800 | tf_op jit(solution)/shard_map/ppermute | solution.py:23
  88.4 1.4 fusion.9
  89.9 1.3 collective-permute-start.9
  91.3 1.8 collective-permute-done.9
  93.2 1.3 collective-permute-start.10
  94.5 4.8 %collective-permute-done.10 = f32[2,64,1,32]{1,3,2,0:T(8,128)S(1)} collective-permute-done((f32[2,64,1,32]{1,3,2,0:T(8,128)S(1)}, f32[2,64,1,32]{1,3,2,0:T(8,128)S(1)}, u32[]{:S(2)}, u32[]{:S(2)}) %collective-permute-start.10) | collective-permute-done | bytes 16416 | tf_op jit(solution)/shard_map/ppermute | solution.py:17
  99.3 0.6 collective-permute-start.11
  99.9 3.0 %collective-permute-done.11 = f32[64,2,1]{0,2,1:T(1,128)S(1)} collective-permute-done((f32[64,2,1]{0,2,1:T(1,128)S(1)}, f32[64,2,1]{0,2,1:T(1,128)S(1)}, u32[]{:S(2)}, u32[]{:S(2)}) %collective-permute-start.11) | collective-permute-done | bytes 544 | tf_op jit(solution)/shard_map/ppermute | solution.py:23
  103.0 5.8 %collective-permute-start.12 = (bf16[64,2,32]{0,2,1:T(8,128)(2,1)S(1)}, bf16[64,2,32]{0,2,1:T(8,128)(2,1)S(1)}, u32[]{:S(2)}, u32[]{:S(2)}) collective-permute-start(bf16[64,2,32]{0,2,1:T(8,128)(2,1)S(1)} %multiply_convert_fusion), channel_id=1, source_target_pairs={{0,1},{1,2},{2,3},{4,5},{5,6},{6,7},{8,9},{9,10},{10,11},{12,13},{... | collective-permute-start | bytes 24584 | tf_op jit(solution)/shard_map/ppermute | solution.py:17
  108.8 0.6 constant_dynamic-update-slice_fusion.23
  109.7 3.6 %collective-permute-start.13 = (bf16[2,64,1,32]{1,3,2,0:T(8,128)(2,1)S(1)}, bf16[2,64,1,32]{1,3,2,0:T(8,128)(2,1)S(1)}, u32[]{:S(2)}, u32[]{:S(2)}) collective-permute-start(bf16[2,64,1,32]{1,3,2,0:T(8,128)(2,1)S(1)} %pad_maximum_fusion.4), channel_id=1, source_target_pairs={{0,8},{8,16},{16,24},{1,9},{9,17},{17,25},{2,10},{10,18},{18,26},{... | collective-permute-start | bytes 24584 | tf_op jit(solution)/shard_map/ppermute | solution.py:17
  113.3 1.4 collective-permute-done.13
  114.7 0.6 collective-permute-start.14
  115.6 2.8 collective-permute-done.14
  118.8 0.4 fusion.5
  119.3 2.7 multiply_bitcast_fusion
  122.1 7.9 %copy.41 = f32[64,2,78,2,4,2,4]{0,6,5,4,3,2,1:T(4,128)} copy(f32[64,2,78,2,4,2,4]{2,0,5,3,1,6,4:T(8,128)} %multiply_bitcast_fusion) | data formatting | bytes 5111808 | tf_op jit(solution)/shard_map/mul | solution.py:105
  130.0 149.4 %all-reduce.2.cloned.1.call-done = f32[64,9984]{0,1:T(8,128)} async-done(((f32[64,9984]{0,1:T(8,128)}), f32[64,9984]{0,1:T(8,128)}) %all-reduce.2.cloned.1.call-update) | async-done | bytes 2555920 | tf_op jit(solution)/shard_map/psum | solution.py:105
  279.4 4.8 %constant_dynamic-slice_fusion = f32[32,9984]{0,1:T(8,128)} fusion(f32[64,9984]{0,1:T(8,128)} %all-reduce.2.cloned.1.call-done, s32[]{:T(128)S(6)} %select_n.3), kind=kLoop, calls=%fused_computation.87 | loop fusion | bytes 2555908 | tf_op jit(solution)/shard_map/dynamic_slice | solution.py:106
  284.1 4.9 %copy.42 = f32[32,9984]{1,0:T(8,128)} copy(f32[32,9984]{0,1:T(8,128)} %constant_dynamic-slice_fusion) | data formatting | bytes 2555904
  (75 shorter events, 2.6 us)
Async XLA Ops:
  7.2 38.9 %all-gather.2.cloned.1.call-start = ((), (), s32[]{:S(2)}) async-start(), calls=%async_computation | async-start | bytes 1916928 | tf_op jit(solution)/shard_map/all_gather | solution.py:55
  8.0 3.2 %collective-permute-start = (bf16[64,2,32]{0,2,1:T(8,128)(2,1)S(1)}, bf16[64,2,32]{0,2,1:T(8,128)(2,1)S(1)}, u32[]{:S(2)}, u32[]{:S(2)}) collective-permute-start(bf16[64,2,32]{0,2,1:T(8,128)(2,1)S(1)} %bitcast_convert_fusion), channel_id=1, source_target_pairs={{0,1},{1,2},{2,3},{4,5},{5,6},{6,7},{8,9},{9,10},{10,11},{12,13},{... | collective-permute-start | bytes 24584 | tf_op jit(solution)/shard_map/ppermute | solution.py:17
  11.2 5.7 %collective-permute-start.1 = (bf16[2,64,1,32]{1,3,2,0:T(8,128)(2,1)S(1)}, bf16[2,64,1,32]{1,3,2,0:T(8,128)(2,1)S(1)}, u32[]{:S(2)}, u32[]{:S(2)}) collective-permute-start(bf16[2,64,1,32]{1,3,2,0:T(8,128)(2,1)S(1)} %pad_maximum_fusion.10), channel_id=1, source_target_pairs={{0,8},{8,16},{16,24},{1,9},{9,17},{17,25},{2,10},{10,18},{18,26},{... | collective-permute-start | bytes 24584 | tf_op jit(solution)/shard_map/ppermute | solution.py:17
  16.9 4.9 %collective-permute-start.2 = (bf16[2,64,3,1]{1,3,2,0:T(2,128)(2,1)S(1)}, bf16[2,64,3,1]{1,3,2,0:T(2,128)(2,1)S(1)}, u32[]{:S(2)}, u32[]{:S(2)}) collective-permute-start(bf16[2,64,3,1]{1,3,2,0:T(2,128)(2,1)S(1)} %pad_maximum_fusion.13), channel_id=1, source_target_pairs={{4,0},{0,4},{5,1},{1,5},{6,2},{2,6},{7,3},{3,7},{12,8},{8,12},{13,... | collective-permute-start | bytes 2312 | tf_op jit(solution)/shard_map/ppermute | solution.py:23
  18.5 260.9 %all-reduce.2.cloned.1.call-start = ((), (), s32[]{:S(2)}) async-start(), calls=%async_computation.1 | async-start | bytes 10223616 | tf_op jit(solution)/shard_map/psum | solution.py:105
  58.1 5.3 %copy-start.3 = (f32[64]{0:T(128)S(1)}, f32[64]{0:T(128)}, u32[]{:S(2)}) copy-start(f32[64]{0:T(128)} %param.7) | copy-start | bytes 772
  61.2 15.0 %copy-start.2 = (f32[1,64,2,32]{1,3,2,0:T(8,128)S(1)}, f32[1,64,2,32]{1,3,2,0:T(8,128)}, u32[]{:S(2)}) copy-start(f32[1,64,2,32]{1,3,2,0:T(8,128)} %param.6) | copy-start | bytes 49156
  61.3 27.0 %copy-start.1 = (bf16[8,64,1248]{2,1,0:T(8,128)(2,1)S(1)}, bf16[8,64,1248]{2,1,0:T(8,128)(2,1)}, u32[]{:S(2)}) copy-start(bf16[8,64,1248]{2,1,0:T(8,128)(2,1)} %copy.23) | copy-start | bytes 3833860
  62.0 26.4 %copy-start = (bf16[1248,8,64]{0,2,1:T(8,128)(2,1)S(1)}, bf16[1248,8,64]{0,2,1:T(8,128)(2,1)}, u32[]{:S(2)}) copy-start(bf16[1248,8,64]{0,2,1:T(8,128)(2,1)} %copy.20) | copy-start | bytes 3833860
  62.0 3.7 %collective-permute-start.3 = (f32[4,64,2,32]{1,3,0,2:T(8,128)}, f32[4,64,2,32]{1,3,0,2:T(8,128)}, u32[]{:S(2)}, u32[]{:S(2)}) collective-permute-start(f32[4,64,2,32]{1,3,0,2:T(8,128)} %copy.24), channel_id=1, source_target_pairs={{1,0},{2,1},{3,2},{5,4},{6,5},{7,6},{9,8},{10,9},{11,10},{13,12},{... | collective-permute-start | bytes 196616 | tf_op jit(solution)/shard_map/ppermute | solution.py:17
  66.7 5.8 %collective-permute-start.4 = (f32[2,64,1,32]{1,3,0,2:T(8,128)S(1)}, f32[2,64,1,32]{1,3,0,2:T(8,128)S(1)}, u32[]{:S(2)}, u32[]{:S(2)}) collective-permute-start(f32[2,64,1,32]{1,3,0,2:T(8,128)S(1)} %slice_bitcast_fusion.4), channel_id=1, source_target_pairs={{8,0},{16,8},{24,16},{9,1},{17,9},{25,17},{10,2},{18,10},{26,18},{... | collective-permute-start | bytes 49160 | tf_op jit(solution)/shard_map/ppermute | solution.py:17
  72.5 3.6 %collective-permute-start.5 = (f32[64,2,1]{0,2,1:T(1,128)S(1)}, f32[64,2,1]{0,2,1:T(1,128)S(1)}, u32[]{:S(2)}, u32[]{:S(2)}) collective-permute-start(f32[64,2,1]{0,2,1:T(1,128)S(1)} %slice_bitcast_fusion.7), channel_id=1, source_target_pairs={{4,0},{0,4},{5,1},{1,5},{6,2},{2,6},{7,3},{3,7},{12,8},{8,12},{13,... | collective-permute-start | bytes 1544 | tf_op jit(solution)/shard_map/ppermute | solution.py:23
  76.2 3.3 %collective-permute-start.6 = (bf16[64,2,32]{0,2,1:T(8,128)(2,1)S(1)}, bf16[64,2,32]{0,2,1:T(8,128)(2,1)S(1)}, u32[]{:S(2)}, u32[]{:S(2)}) collective-permute-start(bf16[64,2,32]{0,2,1:T(8,128)(2,1)S(1)} %get-tuple-element.7), channel_id=1, source_target_pairs={{0,1},{1,2},{2,3},{4,5},{5,6},{6,7},{8,9},{9,10},{10,11},{12,13},{... | collective-permute-start | bytes 24584 | tf_op jit(solution)/shard_map/ppermute | solution.py:17
  79.5 4.8 %collective-permute-start.7 = (bf16[2,64,1,32]{1,3,2,0:T(8,128)(2,1)S(1)}, bf16[2,64,1,32]{1,3,2,0:T(8,128)(2,1)S(1)}, u32[]{:S(2)}, u32[]{:S(2)}) collective-permute-start(bf16[2,64,1,32]{1,3,2,0:T(8,128)(2,1)S(1)} %pad_maximum_fusion.7), channel_id=1, source_target_pairs={{0,8},{8,16},{16,24},{1,9},{9,17},{17,25},{2,10},{10,18},{18,26},{... | collective-permute-start | bytes 24584 | tf_op jit(solution)/shard_map/ppermute | solution.py:17
  84.3 3.7 %collective-permute-start.8 = (bf16[2,64,3,1]{1,3,2,0:T(2,128)(2,1)S(1)}, bf16[2,64,3,1]{1,3,2,0:T(2,128)(2,1)S(1)}, u32[]{:S(2)}, u32[]{:S(2)}) collective-permute-start(bf16[2,64,3,1]{1,3,2,0:T(2,128)(2,1)S(1)} %pad_maximum_fusion.12), channel_id=1, source_target_pairs={{4,0},{0,4},{5,1},{1,5},{6,2},{2,6},{7,3},{3,7},{12,8},{8,12},{13,... | collective-permute-start | bytes 2312 | tf_op jit(solution)/shard_map/ppermute | solution.py:23
  89.9 3.2 %collective-permute-start.9 = (f32[4,64,2,32]{1,3,2,0:T(8,128)S(1)}, f32[4,64,2,32]{1,3,2,0:T(8,128)S(1)}, u32[]{:S(2)}, u32[]{:S(2)}) collective-permute-start(f32[4,64,2,32]{1,3,2,0:T(8,128)S(1)} %copy.31), channel_id=1, source_target_pairs={{1,0},{2,1},{3,2},{5,4},{6,5},{7,6},{9,8},{10,9},{11,10},{13,12},{... | collective-permute-start | bytes 196616 | tf_op jit(solution)/shard_map/ppermute | solution.py:17
  93.2 6.1 %collective-permute-start.10 = (f32[2,64,1,32]{1,3,2,0:T(8,128)S(1)}, f32[2,64,1,32]{1,3,2,0:T(8,128)S(1)}, u32[]{:S(2)}, u32[]{:S(2)}) collective-permute-start(f32[2,64,1,32]{1,3,2,0:T(8,128)S(1)} %get-tuple-element.15), channel_id=1, source_target_pairs={{8,0},{16,8},{24,16},{9,1},{17,9},{25,17},{10,2},{18,10},{26,18},{... | collective-permute-start | bytes 49160 | tf_op jit(solution)/shard_map/ppermute | solution.py:17
  99.3 3.6 %collective-permute-start.11 = (f32[64,2,1]{0,2,1:T(1,128)S(1)}, f32[64,2,1]{0,2,1:T(1,128)S(1)}, u32[]{:S(2)}, u32[]{:S(2)}) collective-permute-start(f32[64,2,1]{0,2,1:T(1,128)S(1)} %slice_bitcast_fusion.6), channel_id=1, source_target_pairs={{4,0},{0,4},{5,1},{1,5},{6,2},{2,6},{7,3},{3,7},{12,8},{8,12},{13,... | collective-permute-start | bytes 1544 | tf_op jit(solution)/shard_map/ppermute | solution.py:23
  103.0 6.7 %collective-permute-start.12 = (bf16[64,2,32]{0,2,1:T(8,128)(2,1)S(1)}, bf16[64,2,32]{0,2,1:T(8,128)(2,1)S(1)}, u32[]{:S(2)}, u32[]{:S(2)}) collective-permute-start(bf16[64,2,32]{0,2,1:T(8,128)(2,1)S(1)} %multiply_convert_fusion), channel_id=1, source_target_pairs={{0,1},{1,2},{2,3},{4,5},{5,6},{6,7},{8,9},{9,10},{10,11},{12,13},{... | collective-permute-start | bytes 24584 | tf_op jit(solution)/shard_map/ppermute | solution.py:17
  109.7 5.1 %collective-permute-start.13 = (bf16[2,64,1,32]{1,3,2,0:T(8,128)(2,1)S(1)}, bf16[2,64,1,32]{1,3,2,0:T(8,128)(2,1)S(1)}, u32[]{:S(2)}, u32[]{:S(2)}) collective-permute-start(bf16[2,64,1,32]{1,3,2,0:T(8,128)(2,1)S(1)} %pad_maximum_fusion.4), channel_id=1, source_target_pairs={{0,8},{8,16},{16,24},{1,9},{9,17},{17,25},{2,10},{10,18},{18,26},{... | collective-permute-start | bytes 24584 | tf_op jit(solution)/shard_map/ppermute | solution.py:17
  114.7 3.7 %collective-permute-start.14 = (bf16[2,64,3,1]{1,3,2,0:T(2,128)(2,1)S(1)}, bf16[2,64,3,1]{1,3,2,0:T(2,128)(2,1)S(1)}, u32[]{:S(2)}, u32[]{:S(2)}) collective-permute-start(bf16[2,64,3,1]{1,3,2,0:T(2,128)(2,1)S(1)} %pad_maximum_fusion.11), channel_id=1, source_target_pairs={{4,0},{0,4},{5,1},{1,5},{6,2},{2,6},{7,3},{3,7},{12,8},{8,12},{13,... | collective-permute-start | bytes 2312 | tf_op jit(solution)/shard_map/ppermute | solution.py:23
Sparse Core Ops, SparseCore 0:
  18.6 27.4 all-gather.1
  130.1 149.1 all-reduce.1
where the time goes:
time: 297 us; the launch traced here: 296 us
  waiting for transfers between devices  204 us (69%)
  local copies, waits for them, and re-layouts  35.4 us (12%)
  starting transfers between devices  31.1 us (10%)
  between operations  14.4 us (5%)
  matrix products  7.52 us (3%)
  other arithmetic  3.45 us (1%)
    psum x1, waiting for transfers between devices, body(): lax.psum(to_atoms(local, channels, atoms) * scale, ('lat', 'lon', 'tm'))  149 us
    ppermute x10, starting transfers between devices, passed_along(): return lax.ppermute(shard, axis, pairs)  27.3 us
    all_gather x1, waiting for transfers between devices, body(): gathered = lax.all_gather(dictionary, 'lon', axis=0, tiled=True)  23.9 us
    ppermute x10, waiting for transfers between devices, passed_along(): return lax.ppermute(shard, axis, pairs)  18.6 us
    ppermute x5, waiting for transfers between devices, shifted(): return lax.ppermute(block, axis, route)  12.1 us
    mul x1, local copies, waits for them, and re-layouts, body(): to_atoms(local, channels, atoms) * scale  7.91 us
    unnamed x22, local copies, waits for them, and re-layouts  6.17 us
  transfers between devices with their start and end apart: 17, of which 16 were waited for; matrix products, arithmetic and copies ran while one was open for 2% of the time, Pallas kernels for 0%

commit v1 on v0

v1 whole, which is shorter than its diff:
```python
import functools
import math

import jax
import jax.numpy as jnp
import numpy as np
from jax import lax
from jax.experimental import pallas as pl
from jax.experimental.pallas import tpu as pltpu
from jax.sharding import PartitionSpec as P

ITERS = 2
STEP_SIZE = 0.5
MESH = pl.DeviceIdType.MESH
F32, BF16 = jnp.float32, jnp.bfloat16
COMBOS = [(h, a, b) for h in (0, 1) for a in (0, 1) for b in (0, 1)]
GROUP = 512


def cell_order():
    c, a, u, b, v = np.meshgrid(*[np.arange(n) for n in (8, 2, 4, 2, 4)], indexing="ij")
    source = ((((c * 2 + a) * 4 + u) * 2 + b) * 4 + v).ravel()
    target = ((((a * 2 + b) * 8 + c) * 4 + u) * 4 + v).ravel()
    order = np.zeros((GROUP, GROUP), np.float32)
    order[source, target] = 1.0
    return order


def contract(x, y, dx, dy):
    return lax.dot_general(x, y, (((dx,), (dy,)), ((), ())), preferred_element_type=F32)


def kernel(
    sizes, d_ref, p_ref, x_ref, z0_ref, th_ref, codes_ref, grad_ref,
    dfull, bhat, stage, zext, zs, cbuf, qbuf, acc, moving, current,
    gd, ra, sb, rb, sc, rc, sd, rd, fin,
    dict_s, dict_r, relay_s, relay_r, halo_s, halo_r, adj_s, adj_r,
    a_sem, b_s, b_r, c_sem, d_s, d_r, e_s, e_r, f_sem, g_sem,
):
    n_lat, n_lon, n_tm, atoms, rows, cols, half, padded = sizes
    owned = atoms // n_lon
    lat, lon, tm = lax.axis_index("lat"), lax.axis_index("lon"), lax.axis_index("tm")
    left = 8
    full = left + cols
    groups = padded // 128

    def at(la, lo, t):
        return (la, lo, t)

    def remote(src, dst, send, recv, where):
        return pltpu.make_async_remote_copy(
            src_ref=src, dst_ref=dst, send_sem=send, recv_sem=recv, device_id=where, device_id_type=MESH
        )

    def lon_at(step):
        return lax.rem(lon + step + n_lon, n_lon)

    zext[...] = jnp.zeros_like(zext)
    qbuf[...] = jnp.zeros_like(qbuf)

    def set_codes(turn, p, value):
        zext[turn, 0, 1 + p, left:full, :] = value.astype(BF16).astype(F32)

    for p in range(rows):
        value = z0_ref[p * cols : (p + 1) * cols, :]
        moving[p] = value
        current[p] = value
        set_codes(0, p, value)

    barrier = pltpu.get_barrier_semaphore()
    count = n_lat * n_lon * n_tm
    mine = (lat * n_lon + lon) * n_tm + tm

    def greet(step, carry):
        other = lax.rem(mine + step, count)
        where = (other // (n_lon * n_tm), lax.rem(other // n_tm, n_lon), lax.rem(other, n_tm))
        pl.semaphore_signal(barrier, inc=1, device_id=where, device_id_type=MESH)
        return carry

    lax.fori_loop(1, count, greet, 0)
    pl.semaphore_wait(barrier, count - 1)

    odd = lax.rem(tm, 2)
    upper = tm // 2
    pair = tm + 1 - 2 * odd
    cross = tm + 2 - 4 * upper

    def region(ref, head, da, dl, sender):
        r = (pl.ds(rows if sender else 0, 1)) if da else pl.ds(1, rows)
        c = (pl.ds(full - 8 if sender else 0, 8)) if dl else pl.ds(left, cols)
        return ref.at[head + (r, c)]

    def halo(turn, m):
        dt, da, dl = COMBOS[m]
        copy = remote(
            region(zext, (turn, 0), da, dl, True), region(zext, (turn, dt), da, dl, False),
            halo_s.at[turn, m], halo_r.at[turn, m],
            at(lax.rem(lat + da, n_lat), lon_at(dl), lax.rem(tm + dt, n_tm)),
        )
        sends = (tm + dt < n_tm) & (lat + da < n_lat)
        gets = (tm - dt >= 0) & (lat - da >= 0)
        return copy, sends, gets

    def adjoint(turn, m):
        dt, da, dl = COMBOS[m]
        copy = remote(
            region(cbuf, (turn, dt), da, dl, False), region(qbuf, (turn, dt), da, dl, False),
            adj_s.at[turn, m], adj_r.at[turn, m],
            at(lax.rem(lat - da + n_lat, n_lat), lon_at(-dl), lax.rem(tm - dt + n_tm, n_tm)),
        )
        sends = (tm - dt >= 0) & (lat - da >= 0)
        gets = (tm + dt < n_tm) & (lat + da < n_lat)
        return copy, sends, gets

    def start_all(make, turn):
        for m in range(1, 8):
            copy, sends, _ = make(turn, m)
            pl.when(sends)(copy.start)

    def wait_all(make, turn):
        for m in range(1, 8):
            copy, sends, gets = make(turn, m)
            pl.when(gets)(copy.wait_recv)
            pl.when(sends)(copy.wait_send)

    gathers = []
    for s in range(1, n_lon):
        copy = remote(
            d_ref.at[:, pl.ds(pl.multiple_of(odd * half, 128), half)], dfull.at[lon, odd],
            dict_s.at[s - 1], dict_r.at[s - 1], at(lat, lon_at(s), tm),
        )
        copy.start()
        gathers.append(copy)
    start_all(halo, 0)

    order = p_ref[...]

    def lay_out(load, place):
        for h in (0, 1):
            for g in range(groups):
                width = min(GROUP, half - g * GROUP)
                cells = jnp.dot(load(h, g * GROUP, width), order[:width], preferred_element_type=F32)
                for ab in range(4):
                    place((h * 4 + ab) * atoms, g * 128, cells[:, ab * 128 : (ab + 1) * 128])

    aligned = owned % 16 == 0

    def place_at(owner):
        def place(row, lane, value):
            if aligned:
                start = pl.multiple_of(row + owner * owned, 16)
                bhat[pl.ds(start, owned), lane : lane + 128] = value.astype(BF16)
            else:
                stage[row + owner * owned : row + owner * owned + owned, lane : lane + 128] = value
        return place

    if aligned:
        lay_out(lambda h, lane, width: d_ref[:, h * half + lane : h * half + lane + width], place_at(lon))
    relays = []
    for s in range(1, n_lon):
        source = lon_at(-s)
        gathers[s - 1].wait_recv()
        copy = remote(
            dfull.at[source, odd], dfull.at[source, odd], relay_s.at[s - 1], relay_r.at[s - 1], at(lat, lon, pair)
        )
        copy.start()
        relays.append(copy)
    for s in range(1, n_lon):
        source = lon_at(-s)
        relays[s - 1].wait_recv()
        if aligned:
            lay_out(lambda h, lane, width: dfull[source, h, :, lane : lane + width], place_at(source))
    if not aligned:
        for s in range(1, n_lon):
            gathers[s - 1].wait_send()
            relays[s - 1].wait_send()
        for h in (0, 1):
            dfull[lon, h] = d_ref[:, h * half : (h + 1) * half]
        for owner in range(n_lon):
            lay_out(lambda h, lane, width: dfull[owner, h, :, lane : lane + width], place_at(owner))
        bhat[...] = stage[...].astype(BF16)

    def stack_codes(turn):
        for i, (h, a, b) in enumerate(COMBOS):
            for p in range(rows):
                zs[p * cols : (p + 1) * cols, i * atoms : (i + 1) * atoms] = zext[
                    turn, h, 1 + p - a, left - b : full - b, :
                ]
        return zs[...].astype(BF16)

    def residual(stacked):
        synth = jnp.dot(stacked, bhat[...], preferred_element_type=F32)
        return (synth - x_ref[...].astype(F32)).astype(BF16)

    shrink = STEP_SIZE * th_ref[...]
    momentum = 1.0
    for turn in range(ITERS):
        wait_all(halo, turn)
        resid = residual(stack_codes(turn))
        terms = contract(resid, bhat[...], 1, 1)
        cbuf[turn] = jnp.zeros_like(cbuf[turn])
        for i, (h, a, b) in enumerate(COMBOS):
            for p in range(rows):
                cbuf[turn, h, 1 + p - a, left - b : full - b, :] += terms[
                    p * cols : (p + 1) * cols, i * atoms : (i + 1) * atoms
                ]
        start_all(adjoint, turn)
        wait_all(adjoint, turn)
        later = (1.0 + math.sqrt(1.0 + 4.0 * momentum * momentum)) / 2.0
        weight = (momentum - 1.0) / later
        momentum = later
        for p in range(rows):
            total = cbuf[turn, 0, 1 + p, left:full, :] + qbuf[turn, 1, 1 + p, left:full, :]
            edge = qbuf[turn, 0, 1 + p, 0:8, :] + qbuf[turn, 1, 1 + p, 0:8, :]
            if p == rows - 1:
                total = total + qbuf[turn, 0, 0, left:full, :] + qbuf[turn, 1, 0, left:full, :]
                edge = edge + qbuf[turn, 0, 0, 0:8, :] + qbuf[turn, 1, 0, 0:8, :]
            acc[...] = total
            acc[cols - 8 : cols, :] += edge
            descent = moving[p] - STEP_SIZE * acc[...]
            updated = jnp.where(
                descent > shrink, descent - shrink, jnp.where(descent < -shrink, descent + shrink, 0.0)
            )
            ahead = updated + weight * (updated - current[p])
            moving[p] = ahead
            current[p] = updated
            set_codes(turn + 1, p, ahead if turn < ITERS - 1 else updated)
        start_all(halo, turn + 1)
    for p in range(rows):
        codes_ref[p * cols : (p + 1) * cols, :] = current[p]
    wait_all(halo, ITERS)
    stacked = stack_codes(ITERS)
    resid = residual(stacked)

    for h in (0, 1):
        part = contract(stacked[:, h * 4 * atoms : (h + 1) * 4 * atoms], resid, 0, 0).astype(BF16)
        for g in range(groups):
            cells = jnp.concatenate(
                [part[ab * atoms : (ab + 1) * atoms, g * 128 : (g + 1) * 128] for ab in range(4)], axis=1
            )
            plain = contract(cells, order, 1, 1)
            for j in range(4):
                tile = 4 * g + j
                lane = tile % 5 * 128
                for owner in range(n_lon):
                    gd[h, tile // 5, owner, :, lane : lane + 128] = plain[
                        owner * owned : (owner + 1) * owned, j * 128 : (j + 1) * 128
                    ].astype(BF16)

    copy = remote(gd.at[1 - odd], ra, a_sem.at[0], a_sem.at[1], at(lat, lon, pair))
    copy.start()
    copy.wait()
    sb[...] = (gd[odd].astype(F32) + ra[...].astype(F32)).astype(BF16)
    copies = []
    for s in range(1, n_lon):
        copy = remote(sb.at[:, lon_at(s)], rb.at[s - 1], b_s.at[s - 1], b_r.at[s - 1], at(lat, lon_at(s), tm))
        copy.start()
        copies.append(copy)
    total = sb[:, lon].astype(F32)
    for s in range(1, n_lon):
        copies[s - 1].wait()
        total = total + rb[s - 1].astype(F32)
    sc[...] = total.astype(BF16)
    copy = remote(sc.at[pl.ds((1 - upper) * 4, 4)], rc, c_sem.at[0], c_sem.at[1], at(lat, lon, cross))
    copy.start()
    copy.wait()
    sd[...] = (sc[pl.ds(upper * 4, 4)].astype(F32) + rc[...].astype(F32)).astype(BF16)
    copies = []
    for s in range(1, n_lat):
        to = lax.rem(lat + s, n_lat)
        copy = remote(sd.at[to], rd.at[s - 1], d_s.at[s - 1], d_r.at[s - 1], at(to, lon, tm))
        copy.start()
        copies.append(copy)
    total = sd[lat].astype(F32)
    for s in range(1, n_lat):
        copies[s - 1].wait()
        total = total + rd[s - 1].astype(F32)
    eighth = upper * 4 + lat
    fin[odd, eighth] = total.astype(BF16)
    copies = []
    for s in range(1, n_lat):
        to = lax.rem(lat + s, n_lat)
        copy = remote(
            fin.at[odd, eighth], fin.at[odd, eighth], e_s.at[s - 1], e_r.at[s - 1], at(to, lon, tm)
        )
        copy.start()
        copies.append(copy)
    for copy in copies:
        copy.wait()
    four = fin.at[odd, pl.ds(upper * 4, 4)]
    copy = remote(four, four, f_sem.at[0], f_sem.at[1], at(lat, lon, cross))
    copy.start()
    copy.wait()
    copy = remote(fin.at[odd], fin.at[odd], g_sem.at[0], g_sem.at[1], at(lat, lon, pair))
    copy.start()
    copy.wait()
    for h in (0, 1):
        for eighth in range(8):
            width = min(640, half - eighth * 640)
            lane = h * half + eighth * 640
            grad_ref[:, lane : lane + width] = fin[h, eighth, :, :width]
    if aligned:
        for s in range(1, n_lon):
            gathers[s - 1].wait_send()
            relays[s - 1].wait_send()


def body(sizes, signal, dictionary, codes_init, thresholds):
    n_lat, n_lon, n_tm, atoms, rows, cols, half, padded = sizes
    channels = signal.shape[1]
    patch = channels * 16
    positions = rows * cols
    owned = dictionary.shape[0]
    target = signal[0].reshape(channels, rows, 4, cols, 4).transpose(1, 3, 0, 2, 4).reshape(positions, patch)
    target = jnp.pad(target, ((0, 0), (0, padded - patch)))
    start = codes_init[0].reshape(atoms, positions).T
    order = jnp.asarray(cell_order(), BF16)
    ext = (2, rows + 1, 8 + cols, atoms)
    dma = pltpu.SemaphoreType.DMA
    codes, grad = pl.pallas_call(
        functools.partial(kernel, sizes),
        out_shape=(
            jax.ShapeDtypeStruct((positions, atoms), F32),
            jax.ShapeDtypeStruct(dictionary.shape, BF16),
        ),
        in_specs=[pl.BlockSpec(memory_space=pltpu.VMEM)] * 5,
        out_specs=(pl.BlockSpec(memory_space=pltpu.VMEM),) * 2,
        scratch_shapes=[
            pltpu.VMEM((n_lon, 2, owned, half), BF16),
            pltpu.VMEM((8 * atoms, padded), BF16),
            pltpu.VMEM((8, 128) if owned % 16 == 0 else (8 * atoms, padded), F32),
            pltpu.VMEM((ITERS + 1,) + ext, F32),
            pltpu.VMEM((positions, 8 * atoms), F32),
            pltpu.VMEM((ITERS,) + ext, F32),
            pltpu.VMEM((ITERS,) + ext, F32),
            pltpu.VMEM((cols, atoms), F32),
            pltpu.VMEM((rows, cols, atoms), F32),
            pltpu.VMEM((rows, cols, atoms), F32),
            pltpu.VMEM((2, 8, n_lon, owned, 640), BF16),
            pltpu.VMEM((8, n_lon, owned, 640), BF16),
            pltpu.VMEM((8, n_lon, owned, 640), BF16),
            pltpu.VMEM((n_lon - 1, 8, owned, 640), BF16),
            pltpu.VMEM((8, owned, 640), BF16),
            pltpu.VMEM((4, owned, 640), BF16),
            pltpu.VMEM((4, owned, 640), BF16),
            pltpu.VMEM((n_lat - 1, owned, 640), BF16),
            pltpu.VMEM((2, 8, owned, 640), BF16),
            dma((n_lon - 1,)), dma((n_lon - 1,)), dma((n_lon - 1,)), dma((n_lon - 1,)),
            dma((ITERS + 1, 8)), dma((ITERS + 1, 8)), dma((ITERS, 8)), dma((ITERS, 8)),
            dma((2,)), dma((n_lon - 1,)), dma((n_lon - 1,)), dma((2,)),
            dma((n_lat - 1,)), dma((n_lat - 1,)), dma((n_lat - 1,)), dma((n_lat - 1,)),
            dma((2,)), dma((2,)),
        ],
        compiler_params=pltpu.CompilerParams(
            collective_id=0, has_side_effects=True, vmem_limit_bytes=48 * 2**20
        ),
        cost_estimate=pl.CostEstimate(flops=10**9, bytes_accessed=4 * 10**6, transcendentals=0),
    )(dictionary, order, target, start, thresholds[None, :])
    scale = 1.0 / math.sqrt(n_tm * n_lat * n_lon * positions)
    return codes.T.reshape(1, atoms, rows, cols), grad.astype(F32) * scale


def solution(mesh):
    n_lat, n_lon, n_tm = mesh.shape["lat"], mesh.shape["lon"], mesh.shape["tm"]
    assert n_lat == 4 and n_tm == 4 and n_lon >= 2
    placed = (P("tm", None, "lat", "lon"), P("lon", None), P("tm", None, "lat", "lon"), P())

    def part(signal, dictionary, codes_init, thresholds):
        atoms, rows, cols = codes_init.shape[1:]
        half = dictionary.shape[1] // 2
        sizes = (n_lat, n_lon, n_tm, atoms, rows, cols, half, -(-half // GROUP) * 128)
        return body(sizes, signal, dictionary, codes_init, thresholds)

    return jax.shard_map(
        part,
        mesh=mesh,
        in_specs=placed,
        out_specs=(P("tm", None, "lat", "lon"), P("lon", None)),
        check_vma=False,
    )
```

time: 297 us -> 74.5 us (0.25)
  waiting for transfers between devices: 204 us -> 0 us
  Pallas kernels: 0 us -> 69.6 us
  local copies, waits for them, and re-layouts: 35.4 us -> 2.93 us
  starting transfers between devices: 31.1 us -> 0 us
  between operations: 14.4 us -> 0.72 us
  matrix products: 7.52 us -> 0 us
    psum x1 -> x0, waiting for transfers between devices: 149 us -> none  [body(): lax.psum(to_atoms(local, channels, atoms) * scale, ('lat', 'lon', 'tm'))]
    pallas_call x0 -> x1, Pallas kernels: none -> 69.6 us  [body(): pl.pallas_call(functools.partial(kernel, sizes), out_shape=(jax.ShapeDtyp...]
    ppermute x15 -> x0, starting transfers between devices: 31.1 us -> none  [the longest x10 27.3 us: passed_along(): return lax.ppermute(shard, axis, pairs)]
    ppermute x15 -> x0, waiting for transfers between devices: 30.7 us -> none  [the longest x10 18.6 us: passed_along(): return lax.ppermute(shard, axis, pairs)]
    all_gather x1 -> x0, waiting for transfers between devices: 23.9 us -> none  [body(): gathered = lax.all_gather(dictionary, 'lon', axis=0, tiled=True)]
    mul x1 -> x0, local copies, waits for them, and re-layouts: 7.91 us -> none  [body(): to_atoms(local, channels, atoms) * scale]
    transpose x3 -> x1, local copies, waits for them, and re-layouts: 8.19 us -> 0.66 us  [body(): signal[0].reshape(channels, rows, 4, cols, 4).transpose(1, 3, 0, 2, 4)]
    dot_general x4 -> x0, matrix products: 7.52 us -> none  [the longest x2 4.44 us: body(): jnp.dot(partial_matrix, residual, preferred_element_type=jnp.float32)]
  transfers between devices with their start and end apart: 17 -> 0, of which waited for: 16 -> 0; matrix products, arithmetic and copies ran while one was open for 2% -> 0% of each run, Pallas kernels for 0% -> 0%
where the time goes in v1:
time: 74.5 us; the launch traced here: 74.4 us
  Pallas kernels  69.6 us (93%)
  local copies, waits for them, and re-layouts  2.93 us (4%)
  other arithmetic  1.14 us (2%)
    pallas_call x1, Pallas kernels, body(): pl.pallas_call(functools.partial(kernel, sizes), out_shape=(jax.ShapeDtyp...  69.6 us
    unnamed x10, local copies, waits for them, and re-layouts  1.8 us

profile of v1, /device:TPU:0, one launch (start us, length us, event | category | flops | bytes accessed | tf_op | source)
XLA Modules:
  0.0 74.4 jit_solution(523615559048799483)
XLA Ops:
  0.6 1.1 %copy.8 = bf16[1,78,8,128]{1,3,2,0:T(8,128)(2,1)S(1)} copy(bf16[1,78,8,128]{3,2,1,0:T(8,128)(2,1)} %param.5) | data formatting | bytes 319488 | tf_op args[0]
  1.8 0.0 copy-start
  1.8 0.0 copy-start.1
  1.8 0.0 copy-start.2
  1.8 0.0 copy-start.3
  1.8 0.7 copy.9
  2.5 0.3 reshape.10
  2.8 0.2 copy.10
  3.0 0.0 copy-done
  3.0 0.0 copy-done.1
  3.0 0.0 copy-done.2
  3.0 0.0 copy-done.3
  3.0 69.6 %shard_map.68 = (f32[64,64]{1,0:T(8,128)S(1)}, bf16[32,9984]{1,0:T(8,128)(2,1)S(1)}) custom-call(bf16[32,9984]{1,0:T(8,128)(2,1)S(1)} %copy-done, bf16[512,512]{1,0:T(8,128)(2,1)S(1)} %copy-done.3, bf16[64,1280]{1,0:T(8,128)(2,1)S(1)} %pad.4.x_ref, f32[64,64]{1,0:T(8,128)S(1)} %bitcast.13, f32[1,64]{1,0:T(1,128)S(1)} %bitcast.14), custom_call_target="tpu_custom_call" | custom-call | flops 1000000000 | bytes 4000000 | tf_op jit(solution)/shard_map/pallas_call | solution.py:320
  72.6 1.1 %convert_multiply_fusion = f32[32,9984]{1,0:T(8,128)} fusion(bf16[32,9984]{1,0:T(8,128)(2,1)S(1)} %get-tuple-element.5), kind=kLoop, calls=%fused_computation | loop fusion | flops 638976 | bytes 1916928 | tf_op jit(solution)/shard_map/mul | solution.py:360
  73.7 0.6 copy.12
  (1 shorter events, 0.0 us)
Async XLA Ops:
  1.8 1.2 %copy-start = (bf16[32,9984]{1,0:T(8,128)(2,1)S(1)}, bf16[32,9984]{1,0:T(8,128)(2,1)}, u32[]{:S(2)}) copy-start(bf16[32,9984]{1,0:T(8,128)(2,1)} %d_ref.1) | copy-start | bytes 1916932
  1.8 1.2 %copy-start.1 = (f32[1,64,2,32]{1,3,2,0:T(8,128)S(1)}, f32[1,64,2,32]{1,3,2,0:T(8,128)}, u32[]{:S(2)}) copy-start(f32[1,64,2,32]{1,3,2,0:T(8,128)} %param.7) | copy-start | bytes 49156
  1.8 1.2 %copy-start.2 = (f32[64]{0:T(128)S(1)}, f32[64]{0:T(128)}, u32[]{:S(2)}) copy-start(f32[64]{0:T(128)} %param.8) | copy-start | bytes 772
  1.8 1.2 %copy-start.3 = (bf16[512,512]{1,0:T(8,128)(2,1)S(1)}, bf16[512,512]{1,0:T(8,128)(2,1)}, u32[]{:S(2)}) copy-start(bf16[512,512]{1,0:T(8,128)(2,1)} %constant.7.clone.p_ref) | copy-start | bytes 1572868

commit v2 on v1

--- a/solution.py
+++ b/solution.py
@@ -33,9 +33,9 @@
 def kernel(
     sizes, d_ref, p_ref, x_ref, z0_ref, th_ref, codes_ref, grad_ref,
     dfull, bhat, stage, zext, zs, cbuf, qbuf, acc, moving, current,
-    gd, ra, sb, rb, sc, rc, sd, rd, fin,
+    zh, away, home, ra, sb, rb, sc, rc, sd, rd, fin,
     dict_s, dict_r, relay_s, relay_r, halo_s, halo_r, adj_s, adj_r,
-    a_sem, b_s, b_r, c_sem, d_s, d_r, e_s, e_r, f_sem, g_sem,
+    a_s, a_r, b_s, b_r, c_s, c_r, d_s, d_r, e_s, e_r, f_s, f_r, g_s, g_r,
 ):
     n_lat, n_lon, n_tm, atoms, rows, cols, half, padded = sizes
     owned = atoms // n_lon
@@ -123,61 +123,95 @@
             pl.when(gets)(copy.wait_recv)
             pl.when(sends)(copy.wait_send)
 
-    gathers = []
-    for s in range(1, n_lon):
-        copy = remote(
-            d_ref.at[:, pl.ds(pl.multiple_of(odd * half, 128), half)], dfull.at[lon, odd],
-            dict_s.at[s - 1], dict_r.at[s - 1], at(lat, lon_at(s), tm),
-        )
-        copy.start()
-        gathers.append(copy)
-    start_all(halo, 0)
+    lanes = [(g, min(g + 4, groups)) for g in range(0, groups, 4)]
+    spans = [(g0 * GROUP, min(g1 * GROUP, half)) for g0, g1 in lanes]
+    gathers = {}
+    for c, (first, last) in enumerate(spans):
+        for s in range(1, n_lon):
+            copy = remote(
+                d_ref.at[:, pl.ds(pl.multiple_of(odd * half + first, 128), last - first)],
+                dfull.at[lon, odd, :, pl.ds(first, last - first)],
+                dict_s.at[c, s - 1], dict_r.at[c, s - 1], at(lat, lon_at(s), tm),
+            )
+            copy.start()
+            gathers[c, s] = copy
+        if c == 0:
+            start_all(halo, 0)
 
     order = p_ref[...]
 
-    def lay_out(load, place):
-        for h in (0, 1):
-            for g in range(groups):
-                width = min(GROUP, half - g * GROUP)
-                cells = jnp.dot(load(h, g * GROUP, width), order[:width], preferred_element_type=F32)
-                for ab in range(4):
-                    place((h * 4 + ab) * atoms, g * 128, cells[:, ab * 128 : (ab + 1) * 128])
+    def lay_out(load, place, chunk):
+        g0, g1 = lanes[chunk]
+        pieces = []
+        for g in range(g0, g1):
+            width = min(GROUP, half - g * GROUP)
+            piece = load(g * GROUP, width)
+            if width < GROUP:
+                piece = jnp.concatenate([piece, jnp.zeros((owned, GROUP - width), BF16)], axis=1)
+            pieces.append(piece)
+        cells = jnp.dot(jnp.concatenate(pieces, axis=0), order, preferred_element_type=F32)
+        for g in range(g0, g1):
+            for ab in range(4):
+                place(ab * atoms, g * 128, cells[(g - g0) * owned : (g - g0 + 1) * owned, ab * 128 : (ab + 1) * 128])
 
     aligned = owned % 16 == 0
 
-    def place_at(owner):
+    def place_at(owner, h):
         def place(row, lane, value):
             if aligned:
-                start = pl.multiple_of(row + owner * owned, 16)
+                start = pl.multiple_of(h * 4 * atoms + row + owner * owned, 16)
                 bhat[pl.ds(start, owned), lane : lane + 128] = value.astype(BF16)
             else:
-                stage[row + owner * owned : row + owner * owned + owned, lane : lane + 128] = value
+                start = h * 4 * atoms + row + owner * owned
+                stage[start : start + owned, lane : lane + 128] = value
         return place
 
+    def lay_out_small(owner, h, chunk):
+        for g in range(*lanes[chunk]):
+            width = min(GROUP, half - g * GROUP)
+            cells = jnp.dot(held(owner, h)(g * GROUP, width), order[:width], preferred_element_type=F32)
+            for ab in range(4):
+                place_at(owner, h)(ab * atoms, g * 128, cells[:, ab * 128 : (ab + 1) * 128])
+
+    def held(owner, h):
+        return lambda lane, width: dfull[owner, h, :, lane : lane + width]
+
     if aligned:
-        lay_out(lambda h, lane, width: d_ref[:, h * half + lane : h * half + lane + width], place_at(lon))
-    relays = []
-    for s in range(1, n_lon):
-        source = lon_at(-s)
-        gathers[s - 1].wait_recv()
-        copy = remote(
-            dfull.at[source, odd], dfull.at[source, odd], relay_s.at[s - 1], relay_r.at[s - 1], at(lat, lon, pair)
-        )
-        copy.start()
-        relays.append(copy)
-    for s in range(1, n_lon):
-        source = lon_at(-s)
-        relays[s - 1].wait_recv()
-        if aligned:
-            lay_out(lambda h, lane, width: dfull[source, h, :, lane : lane + width], place_at(source))
+        for c in range(len(lanes)):
+            for h in (0, 1):
+                lay_out(
+                    lambda lane, width: d_ref[:, h * half + lane : h * half + lane + width], place_at(lon, h), c
+                )
+    relays = {}
+
+    def relayed(c):
+        for s in range(1, n_lon):
+            source = lon_at(-s)
+            relays[c, s].wait_recv()
+            if aligned:
+                lay_out(held(source, 1 - odd), place_at(source, 1 - odd), c)
+
+    for c, (first, last) in enumerate(spans):
+        for s in range(1, n_lon):
+            source = lon_at(-s)
+            gathers[c, s].wait_recv()
+            part = dfull.at[source, odd, :, pl.ds(first, last - first)]
+            copy = remote(part, part, relay_s.at[c, s - 1], relay_r.at[c, s - 1], at(lat, lon, pair))
+            copy.start()
+            relays[c, s] = copy
+            if aligned:
+                lay_out(held(source, odd), place_at(source, odd), c)
+        if c > 0:
+            relayed(c - 1)
+    relayed(len(lanes) - 1)
     if not aligned:
-        for s in range(1, n_lon):
-            gathers[s - 1].wait_send()
-            relays[s - 1].wait_send()
+        for copy in [*gathers.values(), *relays.values()]:
+            copy.wait_send()
         for h in (0, 1):
             dfull[lon, h] = d_ref[:, h * half : (h + 1) * half]
-        for owner in range(n_lon):
-            lay_out(lambda h, lane, width: dfull[owner, h, :, lane : lane + width], place_at(owner))
+            for c in range(len(lanes)):
+                for owner in range(n_lon):
+                    lay_out_small(owner, h, c)
         bhat[...] = stage[...].astype(BF16)
 
     def stack_codes(turn):
@@ -232,77 +266,107 @@
     stacked = stack_codes(ITERS)
     resid = residual(stacked)
 
+    wide = 4 * atoms
+    chunks = groups // 2
     for h in (0, 1):
-        part = contract(stacked[:, h * 4 * atoms : (h + 1) * 4 * atoms], resid, 0, 0).astype(BF16)
-        for g in range(groups):
-            cells = jnp.concatenate(
-                [part[ab * atoms : (ab + 1) * atoms, g * 128 : (g + 1) * 128] for ab in range(4)], axis=1
+        zh[h] = stacked[:, h * wide : (h + 1) * wide]
+    part_of = [resid[:, j * 256 : (j + 1) * 256] for j in range(chunks)]
+    pairs = []
+    for j in range(chunks):
+        away[j] = contract(zh[1 - odd], part_of[j], 0, 0)
+        copy = remote(away.at[j], ra.at[j], a_s.at[j], a_r.at[j], at(lat, lon, pair))
+        copy.start()
+        pairs.append(copy)
+    for j in range(chunks):
+        home[j] = contract(zh[odd], part_of[j], 0, 0)
+    eighth = upper * 4 + lat
+
+    def lon_stage(j):
+        pairs[j].wait()
+        part = (home[j] + ra[j]).astype(BF16)
+        cells = jnp.concatenate(
+            [
+                jnp.concatenate(
+                    [part[ab * atoms : (ab + 1) * atoms, g * 128 : (g + 1) * 128] for ab in range(4)], axis=1
+                )
+                for g in (0, 1)
+            ],
+            axis=0,
+        )
+        plain = contract(cells, order, 1, 1)
+        for tile in range(8):
+            row, lane = tile // 4 * atoms, tile % 4 * 128
+            for owner in range(n_lon):
+                sb[j, tile, owner] = plain[
+                    row + owner * owned : row + (owner + 1) * owned, lane : lane + 128
+                ].astype(BF16)
+        return [
+            remote(
+                sb.at[j, :, lon_at(s)], rb.at[s - 1, j], b_s.at[j, s - 1], b_r.at[j, s - 1], at(lat, lon_at(s), tm)
             )
-            plain = contract(cells, order, 1, 1)
-            for j in range(4):
-                tile = 4 * g + j
-                lane = tile % 5 * 128
-                for owner in range(n_lon):
-                    gd[h, tile // 5, owner, :, lane : lane + 128] = plain[
-                        owner * owned : (owner + 1) * owned, j * 128 : (j + 1) * 128
-                    ].astype(BF16)
-
-    copy = remote(gd.at[1 - odd], ra, a_sem.at[0], a_sem.at[1], at(lat, lon, pair))
-    copy.start()
-    copy.wait()
-    sb[...] = (gd[odd].astype(F32) + ra[...].astype(F32)).astype(BF16)
-    copies = []
-    for s in range(1, n_lon):
-        copy = remote(sb.at[:, lon_at(s)], rb.at[s - 1], b_s.at[s - 1], b_r.at[s - 1], at(lat, lon_at(s), tm))
-        copy.start()
-        copies.append(copy)
-    total = sb[:, lon].astype(F32)
-    for s in range(1, n_lon):
-        copies[s - 1].wait()
-        total = total + rb[s - 1].astype(F32)
-    sc[...] = total.astype(BF16)
-    copy = remote(sc.at[pl.ds((1 - upper) * 4, 4)], rc, c_sem.at[0], c_sem.at[1], at(lat, lon, cross))
-    copy.start()
-    copy.wait()
-    sd[...] = (sc[pl.ds(upper * 4, 4)].astype(F32) + rc[...].astype(F32)).astype(BF16)
-    copies = []
-    for s in range(1, n_lat):
-        to = lax.rem(lat + s, n_lat)
-        copy = remote(sd.at[to], rd.at[s - 1], d_s.at[s - 1], d_r.at[s - 1], at(to, lon, tm))
-        copy.start()
-        copies.append(copy)
-    total = sd[lat].astype(F32)
-    for s in range(1, n_lat):
-        copies[s - 1].wait()
-        total = total + rd[s - 1].astype(F32)
-    eighth = upper * 4 + lat
-    fin[odd, eighth] = total.astype(BF16)
-    copies = []
-    for s in range(1, n_lat):
-        to = lax.rem(lat + s, n_lat)
-        copy = remote(
-            fin.at[odd, eighth], fin.at[odd, eighth], e_s.at[s - 1], e_r.at[s - 1], at(to, lon, tm)
-        )
-        copy.start()
-        copies.append(copy)
-    for copy in copies:
-        copy.wait()
-    four = fin.at[odd, pl.ds(upper * 4, 4)]
-    copy = remote(four, four, f_sem.at[0], f_sem.at[1], at(lat, lon, cross))
-    copy.start()
-    copy.wait()
-    copy = remote(fin.at[odd], fin.at[odd], g_sem.at[0], g_sem.at[1], at(lat, lon, pair))
-    copy.start()
-    copy.wait()
-    for h in (0, 1):
-        for eighth in range(8):
-            width = min(640, half - eighth * 640)
-            lane = h * half + eighth * 640
-            grad_ref[:, lane : lane + width] = fin[h, eighth, :, :width]
+            for s in range(1, n_lon)
+        ]
+
+    def cross_stage(j):
+        total = sb[j, :, lon].astype(F32)
+        for s in range(1, n_lon):
+            total = total + rb[s - 1, j].astype(F32)
+        sc[j] = total.astype(BF16)
+        return [
+            remote(sc.at[j, pl.ds((1 - upper) * 4, 4)], rc.at[j], c_s.at[j], c_r.at[j], at(lat, lon, cross))
+        ]
+
+    def lat_stage(j):
+        sd[j] = (sc[j, pl.ds(upper * 4, 4)].astype(F32) + rc[j].astype(F32)).astype(BF16)
+        copies = []
+        for s in range(1, n_lat):
+            to = lax.rem(lat + s, n_lat)
+            copies.append(
+                remote(sd.at[j, to], rd.at[s - 1, j], d_s.at[j, s - 1], d_r.at[j, s - 1], at(to, lon, tm))
+            )
+        return copies
+
+    def lat_back(j):
+        total = sd[j, lat].astype(F32)
+        for s in range(1, n_lat):
+            total = total + rd[s - 1, j].astype(F32)
+        fin[odd, j, eighth] = total.astype(BF16)
+        own = fin.at[odd, j, eighth]
+        return [
+            remote(own, own, e_s.at[j, s - 1], e_r.at[j, s - 1], at(lax.rem(lat + s, n_lat), lon, tm))
+            for s in range(1, n_lat)
+        ]
+
+    def cross_back(j):
+        own = fin.at[odd, j, pl.ds(upper * 4, 4)]
+        return [remote(own, own, f_s.at[j], f_r.at[j], at(lat, lon, cross))]
+
+    def pair_back(j):
+        own = fin.at[odd, j]
+        return [remote(own, own, g_s.at[j], g_r.at[j], at(lat, lon, pair))]
+
+    def finish(j):
+        for h in (0, 1):
+            for tile in range(8):
+                lane = (8 * j + tile) * 128
+                if lane < half:
+                    grad_ref[:, h * half + lane : h * half + lane + 128] = fin[h, j, tile]
+        return []
+
+    stages = [lon_stage, cross_stage, lat_stage, lat_back, cross_back, pair_back, finish]
+    flying = {}
+    for step in range(chunks + len(stages) - 1):
+        for number in reversed(range(len(stages))):
+            j = step - number
+            if 0 <= j < chunks:
+                for copy in flying.get(j, []):
+                    copy.wait()
+                flying[j] = stages[number](j)
+                for copy in flying[j]:
+                    copy.start()
     if aligned:
-        for s in range(1, n_lon):
-            gathers[s - 1].wait_send()
-            relays[s - 1].wait_send()
+        for copy in [*gathers.values(), *relays.values()]:
+            copy.wait_send()
 
 
 def body(sizes, signal, dictionary, codes_init, thresholds):
@@ -317,6 +381,7 @@
     order = jnp.asarray(cell_order(), BF16)
     ext = (2, rows + 1, 8 + cols, atoms)
     dma = pltpu.SemaphoreType.DMA
+    chunks, spans = padded // 256, -(-padded // 512)
     codes, grad = pl.pallas_call(
         functools.partial(kernel, sizes),
         out_shape=(
@@ -336,20 +401,23 @@
             pltpu.VMEM((cols, atoms), F32),
             pltpu.VMEM((rows, cols, atoms), F32),
             pltpu.VMEM((rows, cols, atoms), F32),
-            pltpu.VMEM((2, 8, n_lon, owned, 640), BF16),
-            pltpu.VMEM((8, n_lon, owned, 640), BF16),
-            pltpu.VMEM((8, n_lon, owned, 640), BF16),
-            pltpu.VMEM((n_lon - 1, 8, owned, 640), BF16),
-            pltpu.VMEM((8, owned, 640), BF16),
-            pltpu.VMEM((4, owned, 640), BF16),
-            pltpu.VMEM((4, owned, 640), BF16),
-            pltpu.VMEM((n_lat - 1, owned, 640), BF16),
-            pltpu.VMEM((2, 8, owned, 640), BF16),
-            dma((n_lon - 1,)), dma((n_lon - 1,)), dma((n_lon - 1,)), dma((n_lon - 1,)),
+            pltpu.VMEM((2, positions, 4 * atoms), BF16),
+            pltpu.VMEM((chunks, 4 * atoms, 256), F32),
+            pltpu.VMEM((chunks, 4 * atoms, 256), F32),
+            pltpu.VMEM((chunks, 4 * atoms, 256), F32),
+            pltpu.VMEM((chunks, 8, n_lon, owned, 128), BF16),
+            pltpu.VMEM((n_lon - 1, chunks, 8, owned, 128), BF16),
+            pltpu.VMEM((chunks, 8, owned, 128), BF16),
+            pltpu.VMEM((chunks, 4, owned, 128), BF16),
+            pltpu.VMEM((chunks, 4, owned, 128), BF16),
+            pltpu.VMEM((n_lat - 1, chunks, owned, 128), BF16),
+            pltpu.VMEM((2, chunks, 8, owned, 128), BF16),
+            dma((spans, n_lon - 1)), dma((spans, n_lon - 1)), dma((spans, n_lon - 1)), dma((spans, n_lon - 1)),
             dma((ITERS + 1, 8)), dma((ITERS + 1, 8)), dma((ITERS, 8)), dma((ITERS, 8)),
-            dma((2,)), dma((n_lon - 1,)), dma((n_lon - 1,)), dma((2,)),
-            dma((n_lat - 1,)), dma((n_lat - 1,)), dma((n_lat - 1,)), dma((n_lat - 1,)),
-            dma((2,)), dma((2,)),
+            dma((chunks,)), dma((chunks,)), dma((chunks, n_lon - 1)), dma((chunks, n_lon - 1)),
+            dma((chunks,)), dma((chunks,)),
+            dma((chunks, n_lat - 1)), dma((chunks, n_lat - 1)), dma((chunks, n_lat - 1)), dma((chunks, n_lat - 1)),
+            dma((chunks,)), dma((chunks,)), dma((chunks,)), dma((chunks,)),
         ],
         compiler_params=pltpu.CompilerParams(
             collective_id=0, has_side_effects=True, vmem_limit_bytes=48 * 2**20

time: 74.5 us -> 74.1 us (level)
  no operation moved by 1% of the time
where the time goes in v2:
time: 74.1 us; the launch traced here: 73.9 us
  Pallas kernels  69.1 us (93%)
  local copies, waits for them, and re-layouts  2.93 us (4%)
  other arithmetic  1.14 us (2%)
    pallas_call x1, Pallas kernels, body(): pl.pallas_call(functools.partial(kernel, sizes), out_shape=(jax.ShapeDtyp...  69.1 us
    unnamed x10, local copies, waits for them, and re-layouts  1.8 us

profile of v2, /device:TPU:0, one launch (start us, length us, event | category | flops | bytes accessed | tf_op | source)
XLA Modules:
  0.0 73.9 jit_solution(12202012471123529507)
XLA Ops:
  0.6 1.1 %copy.8 = bf16[1,78,8,128]{1,3,2,0:T(8,128)(2,1)S(1)} copy(bf16[1,78,8,128]{3,2,1,0:T(8,128)(2,1)} %param.5) | data formatting | bytes 319488 | tf_op args[0]
  1.8 0.0 copy-start
  1.8 0.0 copy-start.1
  1.8 0.0 copy-start.2
  1.8 0.0 copy-start.3
  1.8 0.7 copy.9
  2.5 0.3 reshape.10
  2.8 0.2 copy.10
  3.0 0.0 copy-done
  3.0 0.0 copy-done.1
  3.0 0.0 copy-done.2
  3.0 0.0 copy-done.3
  3.0 69.1 %shard_map.68 = (f32[64,64]{1,0:T(8,128)S(1)}, bf16[32,9984]{1,0:T(8,128)(2,1)S(1)}) custom-call(bf16[32,9984]{1,0:T(8,128)(2,1)S(1)} %copy-done, bf16[512,512]{1,0:T(8,128)(2,1)S(1)} %copy-done.3, bf16[64,1280]{1,0:T(8,128)(2,1)S(1)} %pad.4.x_ref, f32[64,64]{1,0:T(8,128)S(1)} %bitcast.13, f32[1,64]{1,0:T(1,128)S(1)} %bitcast.14), custom_call_target="tpu_custom_call" | custom-call | flops 1000000000 | bytes 4000000 | tf_op jit(solution)/shard_map/pallas_call | solution.py:385
  72.2 1.1 %convert_multiply_fusion = f32[32,9984]{1,0:T(8,128)} fusion(bf16[32,9984]{1,0:T(8,128)(2,1)S(1)} %get-tuple-element.5), kind=kLoop, calls=%fused_computation | loop fusion | flops 638976 | bytes 1916928 | tf_op jit(solution)/shard_map/mul | solution.py:428
  73.3 0.6 copy.12
  (1 shorter events, 0.0 us)
Async XLA Ops:
  1.8 1.2 %copy-start = (bf16[32,9984]{1,0:T(8,128)(2,1)S(1)}, bf16[32,9984]{1,0:T(8,128)(2,1)}, u32[]{:S(2)}) copy-start(bf16[32,9984]{1,0:T(8,128)(2,1)} %d_ref.1) | copy-start | bytes 1916932
  1.8 1.2 %copy-start.1 = (f32[1,64,2,32]{1,3,2,0:T(8,128)S(1)}, f32[1,64,2,32]{1,3,2,0:T(8,128)}, u32[]{:S(2)}) copy-start(f32[1,64,2,32]{1,3,2,0:T(8,128)} %param.7) | copy-start | bytes 49156
  1.8 1.2 %copy-start.2 = (f32[64]{0:T(128)S(1)}, f32[64]{0:T(128)}, u32[]{:S(2)}) copy-start(f32[64]{0:T(128)} %param.8) | copy-start | bytes 772
  1.8 1.2 %copy-start.3 = (bf16[512,512]{1,0:T(8,128)(2,1)S(1)}, bf16[512,512]{1,0:T(8,128)(2,1)}, u32[]{:S(2)}) copy-start(bf16[512,512]{1,0:T(8,128)(2,1)} %constant.7.clone.p_ref) | copy-start | bytes 1572868

commit v3 on v2

--- a/solution.py
+++ b/solution.py
@@ -355,15 +355,13 @@
 
     stages = [lon_stage, cross_stage, lat_stage, lat_back, cross_back, pair_back, finish]
     flying = {}
-    for step in range(chunks + len(stages) - 1):
-        for number in reversed(range(len(stages))):
-            j = step - number
-            if 0 <= j < chunks:
-                for copy in flying.get(j, []):
-                    copy.wait()
-                flying[j] = stages[number](j)
-                for copy in flying[j]:
-                    copy.start()
+    for stage in stages:
+        for j in range(chunks):
+            for copy in flying.get(j, []):
+                copy.wait()
+            flying[j] = stage(j)
+            for copy in flying[j]:
+                copy.start()
     if aligned:
         for copy in [*gathers.values(), *relays.values()]:
             copy.wait_send()

time: 74.1 us -> 64.4 us (0.87)
  Pallas kernels: 69.1 us -> 59.5 us
    pallas_call x1, Pallas kernels: 69.1 us -> 59.5 us  [body(): pl.pallas_call(functools.partial(kernel, sizes), out_shape=(jax.ShapeDtyp...]
where the time goes in v3:
time: 64.4 us; the launch traced here: 64.3 us
  Pallas kernels  59.5 us (92%)
  local copies, waits for them, and re-layouts  2.93 us (5%)
  other arithmetic  1.14 us (2%)
  between operations  0.72 us (1%)
    pallas_call x1, Pallas kernels, body(): pl.pallas_call(functools.partial(kernel, sizes), out_shape=(jax.ShapeDtyp...  59.5 us
    unnamed x10, local copies, waits for them, and re-layouts  1.8 us

profile of v3, /device:TPU:0, one launch (start us, length us, event | category | flops | bytes accessed | tf_op | source)
XLA Modules:
  0.0 64.3 jit_solution(6387754274428173765)
XLA Ops:
  0.6 1.1 %copy.8 = bf16[1,78,8,128]{1,3,2,0:T(8,128)(2,1)S(1)} copy(bf16[1,78,8,128]{3,2,1,0:T(8,128)(2,1)} %param.5) | data formatting | bytes 319488 | tf_op args[0]
  1.8 0.0 copy-start
  1.8 0.0 copy-start.1
  1.8 0.0 copy-start.2
  1.8 0.0 copy-start.3
  1.8 0.7 %copy.9 = bf16[2,32,78,4,4]{1,0,4,3,2:T(2,128)(2,1)S(1)} copy(bf16[2,32,78,4,4]{2,4,1,3,0:T(4,128)(2,1)S(1)} %bitcast.15) | data formatting | bytes 319488 | tf_op jit(solution)/shard_map/transpose | solution.py:376
  2.5 0.3 reshape.10
  2.8 0.2 copy.10
  3.0 0.0 copy-done
  3.0 0.0 copy-done.1
  3.0 0.0 copy-done.2
  3.0 0.0 copy-done.3
  3.0 59.5 %shard_map.68 = (f32[64,64]{1,0:T(8,128)S(1)}, bf16[32,9984]{1,0:T(8,128)(2,1)S(1)}) custom-call(bf16[32,9984]{1,0:T(8,128)(2,1)S(1)} %copy-done, bf16[512,512]{1,0:T(8,128)(2,1)S(1)} %copy-done.3, bf16[64,1280]{1,0:T(8,128)(2,1)S(1)} %pad.4.x_ref, f32[64,64]{1,0:T(8,128)S(1)} %bitcast.13, f32[1,64]{1,0:T(1,128)S(1)} %bitcast.14), custom_call_target="tpu_custom_call" | custom-call | flops 1000000000 | bytes 4000000 | tf_op jit(solution)/shard_map/pallas_call | solution.py:383
  62.5 1.1 %convert_multiply_fusion = f32[32,9984]{1,0:T(8,128)} fusion(bf16[32,9984]{1,0:T(8,128)(2,1)S(1)} %get-tuple-element.5), kind=kLoop, calls=%fused_computation | loop fusion | flops 638976 | bytes 1916928 | tf_op jit(solution)/shard_map/mul | solution.py:426
  63.7 0.6 copy.12
  (1 shorter events, 0.0 us)
Async XLA Ops:
  1.8 1.2 %copy-start = (bf16[32,9984]{1,0:T(8,128)(2,1)S(1)}, bf16[32,9984]{1,0:T(8,128)(2,1)}, u32[]{:S(2)}) copy-start(bf16[32,9984]{1,0:T(8,128)(2,1)} %d_ref.1) | copy-start | bytes 1916932
  1.8 1.2 %copy-start.1 = (f32[1,64,2,32]{1,3,2,0:T(8,128)S(1)}, f32[1,64,2,32]{1,3,2,0:T(8,128)}, u32[]{:S(2)}) copy-start(f32[1,64,2,32]{1,3,2,0:T(8,128)} %param.7) | copy-start | bytes 49156
  1.8 1.2 %copy-start.2 = (f32[64]{0:T(128)S(1)}, f32[64]{0:T(128)}, u32[]{:S(2)}) copy-start(f32[64]{0:T(128)} %param.8) | copy-start | bytes 772
  1.8 1.2 %copy-start.3 = (bf16[512,512]{1,0:T(8,128)(2,1)S(1)}, bf16[512,512]{1,0:T(8,128)(2,1)}, u32[]{:S(2)}) copy-start(bf16[512,512]{1,0:T(8,128)(2,1)} %constant.7.clone.p_ref) | copy-start | bytes 1572868

commit v4 on v3

--- a/solution.py
+++ b/solution.py
@@ -14,6 +14,10 @@
 MESH = pl.DeviceIdType.MESH
 F32, BF16 = jnp.float32, jnp.bfloat16
 COMBOS = [(h, a, b) for h in (0, 1) for a in (0, 1) for b in (0, 1)]
+AROUND = sorted(
+    [(t, a, b) for t in (-1, 0, 1) for a in (-1, 0, 1) for b in (-1, 0, 1) if (t, a, b) != (0, 0, 0)],
+    key=lambda e: abs(e[0]) + abs(e[1]) + abs(e[2]),
+)
 GROUP = 512
 
 
@@ -32,7 +36,7 @@
 
 def kernel(
     sizes, d_ref, p_ref, x_ref, z0_ref, th_ref, codes_ref, grad_ref,
-    dfull, bhat, stage, zext, zs, cbuf, qbuf, acc, moving, current,
+    dfull, bhat, stage, zs, cbuf, qbuf, acc, moving, current,
     zh, away, home, ra, sb, rb, sc, rc, sd, rd, fin,
     dict_s, dict_r, relay_s, relay_r, halo_s, halo_r, adj_s, adj_r,
     a_s, a_r, b_s, b_r, c_s, c_r, d_s, d_r, e_s, e_r, f_s, f_r, g_s, g_r,
@@ -55,17 +59,9 @@
     def lon_at(step):
         return lax.rem(lon + step + n_lon, n_lon)
 
-    zext[...] = jnp.zeros_like(zext)
-    qbuf[...] = jnp.zeros_like(qbuf)
-
-    def set_codes(turn, p, value):
-        zext[turn, 0, 1 + p, left:full, :] = value.astype(BF16).astype(F32)
-
+    current[...] = jnp.zeros_like(current)
     for p in range(rows):
-        value = z0_ref[p * cols : (p + 1) * cols, :]
-        moving[p] = value
-        current[p] = value
-        set_codes(0, p, value)
+        current[0, 1 + p, left:full, :] = z0_ref[p * cols : (p + 1) * cols, :]
 
     barrier = pltpu.get_barrier_semaphore()
     count = n_lat * n_lon * n_tm
@@ -90,38 +86,33 @@
         c = (pl.ds(full - 8 if sender else 0, 8)) if dl else pl.ds(left, cols)
         return ref.at[head + (r, c)]
 
-    def halo(turn, m):
+    def halo(m):
         dt, da, dl = COMBOS[m]
         copy = remote(
-            region(zext, (turn, 0), da, dl, True), region(zext, (turn, dt), da, dl, False),
-            halo_s.at[turn, m], halo_r.at[turn, m],
+            region(current, (0,), da, dl, True), region(current, (dt,), da, dl, False), halo_s.at[m], halo_r.at[m],
             at(lax.rem(lat + da, n_lat), lon_at(dl), lax.rem(tm + dt, n_tm)),
         )
         sends = (tm + dt < n_tm) & (lat + da < n_lat)
         gets = (tm - dt >= 0) & (lat - da >= 0)
         return copy, sends, gets
 
+    def facing(et, ea, el, sender):
+        h = pl.ds(0, 2) if et == 0 else pl.ds(1 if (et > 0) == sender else 0, 1)
+        r = pl.ds(0, rows + 1) if ea == 0 else pl.ds(0 if (ea > 0) == sender else rows, 1)
+        c = pl.ds(0, full) if el == 0 else pl.ds(0 if (el > 0) == sender else full - 8, 8)
+        return h, r, c
+
+    def inside(et, ea):
+        return (tm + et >= 0) & (tm + et < n_tm) & (lat + ea >= 0) & (lat + ea < n_lat)
+
     def adjoint(turn, m):
-        dt, da, dl = COMBOS[m]
+        et, ea, el = AROUND[m]
         copy = remote(
-            region(cbuf, (turn, dt), da, dl, False), region(qbuf, (turn, dt), da, dl, False),
+            cbuf.at[(turn,) + facing(et, ea, el, True)], qbuf.at[(turn, m) + facing(et, ea, el, False)],
             adj_s.at[turn, m], adj_r.at[turn, m],
-            at(lax.rem(lat - da + n_lat, n_lat), lon_at(-dl), lax.rem(tm - dt + n_tm, n_tm)),
+            at(lax.rem(lat - ea + n_lat, n_lat), lon_at(-el), lax.rem(tm - et + n_tm, n_tm)),
         )
-        sends = (tm - dt >= 0) & (lat - da >= 0)
-        gets = (tm + dt < n_tm) & (lat + da < n_lat)
-        return copy, sends, gets
-
-    def start_all(make, turn):
-        for m in range(1, 8):
-            copy, sends, _ = make(turn, m)
-            pl.when(sends)(copy.start)
-
-    def wait_all(make, turn):
-        for m in range(1, 8):
-            copy, sends, gets = make(turn, m)
-            pl.when(gets)(copy.wait_recv)
-            pl.when(sends)(copy.wait_send)
+        return copy, inside(-et, -ea), inside(et, ea)
 
     lanes = [(g, min(g + 4, groups)) for g in range(0, groups, 4)]
     spans = [(g0 * GROUP, min(g1 * GROUP, half)) for g0, g1 in lanes]
@@ -136,7 +127,9 @@
             copy.start()
             gathers[c, s] = copy
         if c == 0:
-            start_all(halo, 0)
+            for m in range(1, 8):
+                copy, sends, _ = halo(m)
+                pl.when(sends)(copy.start)
 
     order = p_ref[...]
 
@@ -214,11 +207,11 @@
                     lay_out_small(owner, h, c)
         bhat[...] = stage[...].astype(BF16)
 
-    def stack_codes(turn):
+    def stack_codes(held):
         for i, (h, a, b) in enumerate(COMBOS):
             for p in range(rows):
-                zs[p * cols : (p + 1) * cols, i * atoms : (i + 1) * atoms] = zext[
-                    turn, h, 1 + p - a, left - b : full - b, :
+                zs[p * cols : (p + 1) * cols, i * atoms : (i + 1) * atoms] = held[
+                    h, 1 + p - a, left - b : full - b, :
                 ]
         return zs[...].astype(BF16)
 
@@ -228,9 +221,15 @@
 
     shrink = STEP_SIZE * th_ref[...]
     momentum = 1.0
+    first_hour = jnp.where(tm > 0, 1.0, 0.0)
+    first_band = jnp.where(lat > 0, 1.0, 0.0)
+    for m in range(1, 8):
+        copy, sends, gets = halo(m)
+        pl.when(gets)(copy.wait_recv)
+        pl.when(sends)(copy.wait_send)
+    moving[...] = current[...]
     for turn in range(ITERS):
-        wait_all(halo, turn)
-        resid = residual(stack_codes(turn))
+        resid = residual(stack_codes(moving))
         terms = contract(resid, bhat[...], 1, 1)
         cbuf[turn] = jnp.zeros_like(cbuf[turn])
         for i, (h, a, b) in enumerate(COMBOS):
@@ -238,32 +237,37 @@
                 cbuf[turn, h, 1 + p - a, left - b : full - b, :] += terms[
                     p * cols : (p + 1) * cols, i * atoms : (i + 1) * atoms
                 ]
-        start_all(adjoint, turn)
-        wait_all(adjoint, turn)
+        for m in reversed(range(len(AROUND))):
+            copy, sends, _ = adjoint(turn, m)
+            pl.when(sends)(copy.start)
+        acc[...] = cbuf[turn]
+        for m in range(len(AROUND)):
+            copy, _, gets = adjoint(turn, m)
+
+            def add(copy=copy, m=m):
+                copy.wait_recv()
+                h, r, c = facing(*AROUND[m], False)
+                acc[h, r, c, :] += qbuf[turn, m, h, r, c, :]
+
+            pl.when(gets)(add)
         later = (1.0 + math.sqrt(1.0 + 4.0 * momentum * momentum)) / 2.0
         weight = (momentum - 1.0) / later
         momentum = later
-        for p in range(rows):
-            total = cbuf[turn, 0, 1 + p, left:full, :] + qbuf[turn, 1, 1 + p, left:full, :]
-            edge = qbuf[turn, 0, 1 + p, 0:8, :] + qbuf[turn, 1, 1 + p, 0:8, :]
-            if p == rows - 1:
-                total = total + qbuf[turn, 0, 0, left:full, :] + qbuf[turn, 1, 0, left:full, :]
-                edge = edge + qbuf[turn, 0, 0, 0:8, :] + qbuf[turn, 1, 0, 0:8, :]
-            acc[...] = total
-            acc[cols - 8 : cols, :] += edge
-            descent = moving[p] - STEP_SIZE * acc[...]
-            updated = jnp.where(
-                descent > shrink, descent - shrink, jnp.where(descent < -shrink, descent + shrink, 0.0)
-            )
-            ahead = updated + weight * (updated - current[p])
-            moving[p] = ahead
-            current[p] = updated
-            set_codes(turn + 1, p, ahead if turn < ITERS - 1 else updated)
-        start_all(halo, turn + 1)
+        for h in (0, 1):
+            for r in range(rows + 1):
+                descent = moving[h, r] - STEP_SIZE * acc[h, r]
+                updated = jnp.where(
+                    descent > shrink, descent - shrink, jnp.where(descent < -shrink, descent + shrink, 0.0)
+                )
+                if h:
+                    updated = updated * first_hour
+                if r == 0:
+                    updated = updated * first_band
+                moving[h, r] = updated + weight * (updated - current[h, r])
+                current[h, r] = updated
     for p in range(rows):
-        codes_ref[p * cols : (p + 1) * cols, :] = current[p]
-    wait_all(halo, ITERS)
-    stacked = stack_codes(ITERS)
+        codes_ref[p * cols : (p + 1) * cols, :] = current[0, 1 + p, left:full, :]
+    stacked = stack_codes(current)
     resid = residual(stacked)
 
     wide = 4 * atoms
@@ -362,6 +366,10 @@
             flying[j] = stage(j)
             for copy in flying[j]:
                 copy.start()
+    for turn in range(ITERS):
+        for m in range(len(AROUND)):
+            copy, sends, _ = adjoint(turn, m)
+            pl.when(sends)(copy.wait_send)
     if aligned:
         for copy in [*gathers.values(), *relays.values()]:
             copy.wait_send()
@@ -392,13 +400,12 @@
             pltpu.VMEM((n_lon, 2, owned, half), BF16),
             pltpu.VMEM((8 * atoms, padded), BF16),
             pltpu.VMEM((8, 128) if owned % 16 == 0 else (8 * atoms, padded), F32),
-            pltpu.VMEM((ITERS + 1,) + ext, F32),
             pltpu.VMEM((positions, 8 * atoms), F32),
             pltpu.VMEM((ITERS,) + ext, F32),
-            pltpu.VMEM((ITERS,) + ext, F32),
-            pltpu.VMEM((cols, atoms), F32),
-            pltpu.VMEM((rows, cols, atoms), F32),
-            pltpu.VMEM((rows, cols, atoms), F32),
+            pltpu.VMEM((ITERS, len(AROUND)) + ext, F32),
+            pltpu.VMEM(ext, F32),
+            pltpu.VMEM(ext, F32),
+            pltpu.VMEM(ext, F32),
             pltpu.VMEM((2, positions, 4 * atoms), BF16),
             pltpu.VMEM((chunks, 4 * atoms, 256), F32),
             pltpu.VMEM((chunks, 4 * atoms, 256), F32),
@@ -411,7 +418,7 @@
             pltpu.VMEM((n_lat - 1, chunks, owned, 128), BF16),
             pltpu.VMEM((2, chunks, 8, owned, 128), BF16),
             dma((spans, n_lon - 1)), dma((spans, n_lon - 1)), dma((spans, n_lon - 1)), dma((spans, n_lon - 1)),
-            dma((ITERS + 1, 8)), dma((ITERS + 1, 8)), dma((ITERS, 8)), dma((ITERS, 8)),
+            dma((8,)), dma((8,)), dma((ITERS, len(AROUND))), dma((ITERS, len(AROUND))),
             dma((chunks,)), dma((chunks,)), dma((chunks, n_lon - 1)), dma((chunks, n_lon - 1)),
             dma((chunks,)), dma((chunks,)),
             dma((chunks, n_lat - 1)), dma((chunks, n_lat - 1)), dma((chunks, n_lat - 1)), dma((chunks, n_lat - 1)),

time: 64.4 us -> 62.1 us (0.964)
  Pallas kernels: 59.5 us -> 57.1 us
    pallas_call x1, Pallas kernels: 59.5 us -> 57.1 us  [body(): pl.pallas_call(functools.partial(kernel, sizes), out_shape=(jax.ShapeDtyp...]
where the time goes in v4:
time: 62.1 us; the launch traced here: 61.9 us
  Pallas kernels  57.1 us (92%)
  local copies, waits for them, and re-layouts  2.93 us (5%)
  other arithmetic  1.14 us (2%)
  between operations  0.72 us (1%)
    pallas_call x1, Pallas kernels, body(): pl.pallas_call(functools.partial(kernel, sizes), out_shape=(jax.ShapeDtyp...  57.1 us
    unnamed x10, local copies, waits for them, and re-layouts  1.8 us

profile of v4, /device:TPU:0, one launch (start us, length us, event | category | flops | bytes accessed | tf_op | source)
XLA Modules:
  0.0 61.9 jit_solution(8012910640990015769)
XLA Ops:
  0.6 1.1 %copy.8 = bf16[1,78,8,128]{1,3,2,0:T(8,128)(2,1)S(1)} copy(bf16[1,78,8,128]{3,2,1,0:T(8,128)(2,1)} %param.5) | data formatting | bytes 319488 | tf_op args[0]
  1.8 0.0 copy-start
  1.8 0.0 copy-start.1
  1.8 0.0 copy-start.2
  1.8 0.0 copy-start.3
  1.8 0.7 %copy.9 = bf16[2,32,78,4,4]{1,0,4,3,2:T(2,128)(2,1)S(1)} copy(bf16[2,32,78,4,4]{2,4,1,3,0:T(4,128)(2,1)S(1)} %bitcast.15) | data formatting | bytes 319488 | tf_op jit(solution)/shard_map/transpose | solution.py:384
  2.5 0.3 reshape.10
  2.8 0.2 copy.10
  3.0 0.0 copy-done
  3.0 0.0 copy-done.1
  3.0 0.0 copy-done.2
  3.0 0.0 copy-done.3
  3.0 57.1 %shard_map.68 = (f32[64,64]{1,0:T(8,128)S(1)}, bf16[32,9984]{1,0:T(8,128)(2,1)S(1)}) custom-call(bf16[32,9984]{1,0:T(8,128)(2,1)S(1)} %copy-done, bf16[512,512]{1,0:T(8,128)(2,1)S(1)} %copy-done.3, bf16[64,1280]{1,0:T(8,128)(2,1)S(1)} %pad.4.x_ref, f32[64,64]{1,0:T(8,128)S(1)} %bitcast.13, f32[1,64]{1,0:T(1,128)S(1)} %bitcast.14), custom_call_target="tpu_custom_call" | custom-call | flops 1000000000 | bytes 4000000 | tf_op jit(solution)/shard_map/pallas_call | solution.py:391
  60.2 1.1 %convert_multiply_fusion = f32[32,9984]{1,0:T(8,128)} fusion(bf16[32,9984]{1,0:T(8,128)(2,1)S(1)} %get-tuple-element.5), kind=kLoop, calls=%fused_computation | loop fusion | flops 638976 | bytes 1916928 | tf_op jit(solution)/shard_map/mul | solution.py:433
  61.3 0.6 copy.12
  (1 shorter events, 0.0 us)
Async XLA Ops:
  1.8 1.2 %copy-start = (bf16[32,9984]{1,0:T(8,128)(2,1)S(1)}, bf16[32,9984]{1,0:T(8,128)(2,1)}, u32[]{:S(2)}) copy-start(bf16[32,9984]{1,0:T(8,128)(2,1)} %d_ref.1) | copy-start | bytes 1916932
  1.8 1.2 %copy-start.1 = (f32[1,64,2,32]{1,3,2,0:T(8,128)S(1)}, f32[1,64,2,32]{1,3,2,0:T(8,128)}, u32[]{:S(2)}) copy-start(f32[1,64,2,32]{1,3,2,0:T(8,128)} %param.7) | copy-start | bytes 49156
  1.8 1.2 %copy-start.2 = (f32[64]{0:T(128)S(1)}, f32[64]{0:T(128)}, u32[]{:S(2)}) copy-start(f32[64]{0:T(128)} %param.8) | copy-start | bytes 772
  1.8 1.2 %copy-start.3 = (bf16[512,512]{1,0:T(8,128)(2,1)S(1)}, bf16[512,512]{1,0:T(8,128)(2,1)}, u32[]{:S(2)}) copy-start(bf16[512,512]{1,0:T(8,128)(2,1)} %constant.7.clone.p_ref) | copy-start | bytes 1572868

commit v5 on v4

--- a/solution.py
+++ b/solution.py
@@ -37,9 +37,9 @@
 def kernel(
     sizes, d_ref, p_ref, x_ref, z0_ref, th_ref, codes_ref, grad_ref,
     dfull, bhat, stage, zs, cbuf, qbuf, acc, moving, current,
-    zh, away, home, ra, sb, rb, sc, rc, sd, rd, fin,
+    zh, away, home, ra, sb, rb, sc, home8, rd, fin,
     dict_s, dict_r, relay_s, relay_r, halo_s, halo_r, adj_s, adj_r,
-    a_s, a_r, b_s, b_r, c_s, c_r, d_s, d_r, e_s, e_r, f_s, f_r, g_s, g_r,
+    a_s, a_r, b_s, b_r, d_s, d_r, e_s, e_r, g_s, g_r,
 ):
     n_lat, n_lon, n_tm, atoms, rows, cols, half, padded = sizes
     owned = atoms // n_lon
@@ -311,39 +311,33 @@
             for s in range(1, n_lon)
         ]
 
-    def cross_stage(j):
+    peers = [(t, s) for s in range(n_lat - 1, -1, -1) for t in (1, 0) if (t, s) != (0, 0)]
+
+    def peer(t, s):
+        to = lax.rem(lat + s, n_lat)
+        return (1 - upper if t else upper) * 4 + to, at(to, lon, cross if t else tm)
+
+    def eighths(j):
         total = sb[j, :, lon].astype(F32)
         for s in range(1, n_lon):
             total = total + rb[s - 1, j].astype(F32)
         sc[j] = total.astype(BF16)
-        return [
-            remote(sc.at[j, pl.ds((1 - upper) * 4, 4)], rc.at[j], c_s.at[j], c_r.at[j], at(lat, lon, cross))
-        ]
-
-    def lat_stage(j):
-        sd[j] = (sc[j, pl.ds(upper * 4, 4)].astype(F32) + rc[j].astype(F32)).astype(BF16)
+        home8[j] = sc[j, eighth].astype(F32)
         copies = []
-        for s in range(1, n_lat):
-            to = lax.rem(lat + s, n_lat)
-            copies.append(
-                remote(sd.at[j, to], rd.at[s - 1, j], d_s.at[j, s - 1], d_r.at[j, s - 1], at(to, lon, tm))
-            )
+        for i, (t, s) in enumerate(peers):
+            place, where = peer(t, s)
+            copies.append(remote(sc.at[j, place], rd.at[i, j], d_s.at[j, i], d_r.at[j, i], where))
         return copies
 
-    def lat_back(j):
-        total = sd[j, lat].astype(F32)
-        for s in range(1, n_lat):
-            total = total + rd[s - 1, j].astype(F32)
+    def eighths_back(j):
+        total = home8[j]
+        for i in range(len(peers)):
+            total = total + rd[i, j].astype(F32)
         fin[odd, j, eighth] = total.astype(BF16)
         own = fin.at[odd, j, eighth]
         return [
-            remote(own, own, e_s.at[j, s - 1], e_r.at[j, s - 1], at(lax.rem(lat + s, n_lat), lon, tm))
-            for s in range(1, n_lat)
+            remote(own, own, e_s.at[j, i], e_r.at[j, i], peer(t, s)[1]) for i, (t, s) in enumerate(peers)
         ]
-
-    def cross_back(j):
-        own = fin.at[odd, j, pl.ds(upper * 4, 4)]
-        return [remote(own, own, f_s.at[j], f_r.at[j], at(lat, lon, cross))]
 
     def pair_back(j):
         own = fin.at[odd, j]
@@ -357,7 +351,7 @@
                     grad_ref[:, h * half + lane : h * half + lane + 128] = fin[h, j, tile]
         return []
 
-    stages = [lon_stage, cross_stage, lat_stage, lat_back, cross_back, pair_back, finish]
+    stages = [lon_stage, eighths, eighths_back, pair_back, finish]
     flying = {}
     for stage in stages:
         for j in range(chunks):
@@ -413,16 +407,14 @@
             pltpu.VMEM((chunks, 8, n_lon, owned, 128), BF16),
             pltpu.VMEM((n_lon - 1, chunks, 8, owned, 128), BF16),
             pltpu.VMEM((chunks, 8, owned, 128), BF16),
-            pltpu.VMEM((chunks, 4, owned, 128), BF16),
-            pltpu.VMEM((chunks, 4, owned, 128), BF16),
-            pltpu.VMEM((n_lat - 1, chunks, owned, 128), BF16),
+            pltpu.VMEM((chunks, owned, 128), F32),
+            pltpu.VMEM((7, chunks, owned, 128), BF16),
             pltpu.VMEM((2, chunks, 8, owned, 128), BF16),
             dma((spans, n_lon - 1)), dma((spans, n_lon - 1)), dma((spans, n_lon - 1)), dma((spans, n_lon - 1)),
             dma((8,)), dma((8,)), dma((ITERS, len(AROUND))), dma((ITERS, len(AROUND))),
             dma((chunks,)), dma((chunks,)), dma((chunks, n_lon - 1)), dma((chunks, n_lon - 1)),
+            dma((chunks, 7)), dma((chunks, 7)), dma((chunks, 7)), dma((chunks, 7)),
             dma((chunks,)), dma((chunks,)),
-            dma((chunks, n_lat - 1)), dma((chunks, n_lat - 1)), dma((chunks, n_lat - 1)), dma((chunks, n_lat - 1)),
-            dma((chunks,)), dma((chunks,)), dma((chunks,)), dma((chunks,)),
         ],
         compiler_params=pltpu.CompilerParams(
             collective_id=0, has_side_effects=True, vmem_limit_bytes=48 * 2**20

time: 62.1 us -> 60 us (0.966)
  Pallas kernels: 57.1 us -> 55 us
    pallas_call x1, Pallas kernels: 57.1 us -> 55 us  [body(): pl.pallas_call(functools.partial(kernel, sizes), out_shape=(jax.ShapeDtyp...]
where the time goes in v5:
time: 60 us; the launch traced here: 59.8 us
  Pallas kernels  55 us (92%)
  local copies, waits for them, and re-layouts  2.93 us (5%)
  other arithmetic  1.14 us (2%)
  between operations  0.72 us (1%)
    pallas_call x1, Pallas kernels, body(): pl.pallas_call(functools.partial(kernel, sizes), out_shape=(jax.ShapeDtyp...  55 us
    unnamed x10, local copies, waits for them, and re-layouts  1.8 us

profile of v5, /device:TPU:0, one launch (start us, length us, event | category | flops | bytes accessed | tf_op | source)
XLA Modules:
  0.0 59.8 jit_solution(1826505899054135768)
XLA Ops:
  0.6 1.1 %copy.8 = bf16[1,78,8,128]{1,3,2,0:T(8,128)(2,1)S(1)} copy(bf16[1,78,8,128]{3,2,1,0:T(8,128)(2,1)} %param.5) | data formatting | bytes 319488 | tf_op args[0]
  1.8 0.0 copy-start
  1.8 0.0 copy-start.1
  1.8 0.0 copy-start.2
  1.8 0.0 copy-start.3
  1.8 0.7 %copy.9 = bf16[2,32,78,4,4]{1,0,4,3,2:T(2,128)(2,1)S(1)} copy(bf16[2,32,78,4,4]{2,4,1,3,0:T(4,128)(2,1)S(1)} %bitcast.15) | data formatting | bytes 319488 | tf_op jit(solution)/shard_map/transpose | solution.py:378
  2.5 0.3 reshape.10
  2.8 0.2 copy.10
  3.0 0.0 copy-done
  3.0 0.0 copy-done.1
  3.0 0.0 copy-done.2
  3.0 0.0 copy-done.3
  3.0 55.0 %shard_map.68 = (f32[64,64]{1,0:T(8,128)S(1)}, bf16[32,9984]{1,0:T(8,128)(2,1)S(1)}) custom-call(bf16[32,9984]{1,0:T(8,128)(2,1)S(1)} %copy-done, bf16[512,512]{1,0:T(8,128)(2,1)S(1)} %copy-done.3, bf16[64,1280]{1,0:T(8,128)(2,1)S(1)} %pad.4.x_ref, f32[64,64]{1,0:T(8,128)S(1)} %bitcast.13, f32[1,64]{1,0:T(1,128)S(1)} %bitcast.14), custom_call_target="tpu_custom_call" | custom-call | flops 1000000000 | bytes 4000000 | tf_op jit(solution)/shard_map/pallas_call | solution.py:385
  58.0 1.1 %convert_multiply_fusion = f32[32,9984]{1,0:T(8,128)} fusion(bf16[32,9984]{1,0:T(8,128)(2,1)S(1)} %get-tuple-element.5), kind=kLoop, calls=%fused_computation | loop fusion | flops 638976 | bytes 1916928 | tf_op jit(solution)/shard_map/mul | solution.py:425
  59.2 0.6 %copy.12 = f32[1,64,2,32]{1,3,2,0:T(8,128)} copy(f32[1,64,2,32]{1,3,2,0:T(8,128)S(1)} %bitcast.12) | data formatting | bytes 32768
  (1 shorter events, 0.0 us)
Async XLA Ops:
  1.8 1.2 %copy-start = (bf16[32,9984]{1,0:T(8,128)(2,1)S(1)}, bf16[32,9984]{1,0:T(8,128)(2,1)}, u32[]{:S(2)}) copy-start(bf16[32,9984]{1,0:T(8,128)(2,1)} %d_ref.1) | copy-start | bytes 1916932
  1.8 1.2 %copy-start.1 = (f32[1,64,2,32]{1,3,2,0:T(8,128)S(1)}, f32[1,64,2,32]{1,3,2,0:T(8,128)}, u32[]{:S(2)}) copy-start(f32[1,64,2,32]{1,3,2,0:T(8,128)} %param.7) | copy-start | bytes 49156
  1.8 1.2 %copy-start.2 = (f32[64]{0:T(128)S(1)}, f32[64]{0:T(128)}, u32[]{:S(2)}) copy-start(f32[64]{0:T(128)} %param.8) | copy-start | bytes 772
  1.8 1.2 %copy-start.3 = (bf16[512,512]{1,0:T(8,128)(2,1)S(1)}, bf16[512,512]{1,0:T(8,128)(2,1)}, u32[]{:S(2)}) copy-start(bf16[512,512]{1,0:T(8,128)(2,1)} %constant.7.clone.p_ref) | copy-start | bytes 1572868

commit v6 on v5

--- a/solution.py
+++ b/solution.py
@@ -37,7 +37,7 @@
 def kernel(
     sizes, d_ref, p_ref, x_ref, z0_ref, th_ref, codes_ref, grad_ref,
     dfull, bhat, stage, zs, cbuf, qbuf, acc, moving, current,
-    zh, away, home, ra, sb, rb, sc, home8, rd, fin,
+    zh, away, ra, sb, rb, sc, home8, rd, fin,
     dict_s, dict_r, relay_s, relay_r, halo_s, halo_r, adj_s, adj_r,
     a_s, a_r, b_s, b_r, d_s, d_r, e_s, e_r, g_s, g_r,
 ):
@@ -61,7 +61,7 @@
 
     current[...] = jnp.zeros_like(current)
     for p in range(rows):
-        current[0, 1 + p, left:full, :] = z0_ref[p * cols : (p + 1) * cols, :]
+        current[0, 1 + p, left:full, :] = z0_ref[p]
 
     barrier = pltpu.get_barrier_semaphore()
     count = n_lat * n_lon * n_tm
@@ -266,7 +266,7 @@
                 moving[h, r] = updated + weight * (updated - current[h, r])
                 current[h, r] = updated
     for p in range(rows):
-        codes_ref[p * cols : (p + 1) * cols, :] = current[0, 1 + p, left:full, :]
+        codes_ref[p] = current[0, 1 + p, left:full, :]
     stacked = stack_codes(current)
     resid = residual(stacked)
 
@@ -281,13 +281,12 @@
         copy = remote(away.at[j], ra.at[j], a_s.at[j], a_r.at[j], at(lat, lon, pair))
         copy.start()
         pairs.append(copy)
-    for j in range(chunks):
-        home[j] = contract(zh[odd], part_of[j], 0, 0)
     eighth = upper * 4 + lat
 
     def lon_stage(j):
+        own = contract(zh[odd], part_of[j], 0, 0)
         pairs[j].wait()
-        part = (home[j] + ra[j]).astype(BF16)
+        part = (own + ra[j]).astype(BF16)
         cells = jnp.concatenate(
             [
                 jnp.concatenate(
@@ -377,7 +376,7 @@
     owned = dictionary.shape[0]
     target = signal[0].reshape(channels, rows, 4, cols, 4).transpose(1, 3, 0, 2, 4).reshape(positions, patch)
     target = jnp.pad(target, ((0, 0), (0, padded - patch)))
-    start = codes_init[0].reshape(atoms, positions).T
+    start = codes_init[0].transpose(1, 2, 0)
     order = jnp.asarray(cell_order(), BF16)
     ext = (2, rows + 1, 8 + cols, atoms)
     dma = pltpu.SemaphoreType.DMA
@@ -385,7 +384,7 @@
     codes, grad = pl.pallas_call(
         functools.partial(kernel, sizes),
         out_shape=(
-            jax.ShapeDtypeStruct((positions, atoms), F32),
+            jax.ShapeDtypeStruct((rows, cols, atoms), F32),
             jax.ShapeDtypeStruct(dictionary.shape, BF16),
         ),
         in_specs=[pl.BlockSpec(memory_space=pltpu.VMEM)] * 5,
@@ -401,7 +400,6 @@
             pltpu.VMEM(ext, F32),
             pltpu.VMEM(ext, F32),
             pltpu.VMEM((2, positions, 4 * atoms), BF16),
-            pltpu.VMEM((chunks, 4 * atoms, 256), F32),
             pltpu.VMEM((chunks, 4 * atoms, 256), F32),
             pltpu.VMEM((chunks, 4 * atoms, 256), F32),
             pltpu.VMEM((chunks, 8, n_lon, owned, 128), BF16),
@@ -422,7 +420,7 @@
         cost_estimate=pl.CostEstimate(flops=10**9, bytes_accessed=4 * 10**6, transcendentals=0),
     )(dictionary, order, target, start, thresholds[None, :])
     scale = 1.0 / math.sqrt(n_tm * n_lat * n_lon * positions)
-    return codes.T.reshape(1, atoms, rows, cols), grad.astype(F32) * scale
+    return codes.transpose(2, 0, 1)[None], grad.astype(F32) * scale
 
 
 def solution(mesh):

time: 60 us -> 60 us (level)
  no operation moved by 1% of the time
where the time goes in v6:
time: 60 us; the launch traced here: 59.8 us
  Pallas kernels  55 us (92%)
  local copies, waits for them, and re-layouts  2.93 us (5%)
  other arithmetic  1.14 us (2%)
  between operations  0.72 us (1%)
    pallas_call x1, Pallas kernels, body(): pl.pallas_call(functools.partial(kernel, sizes), out_shape=(jax.ShapeDtyp...  55 us
    unnamed x10, local copies, waits for them, and re-layouts  1.8 us

profile of v6, /device:TPU:0, one launch (start us, length us, event | category | flops | bytes accessed | tf_op | source)
XLA Modules:
  0.0 59.8 jit_solution(1673212484083703084)
XLA Ops:
  0.6 1.1 %copy.8 = bf16[1,78,8,128]{1,3,2,0:T(8,128)(2,1)S(1)} copy(bf16[1,78,8,128]{3,2,1,0:T(8,128)(2,1)} %param.5) | data formatting | bytes 319488 | tf_op args[0]
  1.8 0.0 copy-start
  1.8 0.0 copy-start.1
  1.8 0.0 copy-start.2
  1.8 0.0 copy-start.3
  1.8 0.7 %copy.9 = bf16[2,32,78,4,4]{1,0,4,3,2:T(2,128)(2,1)S(1)} copy(bf16[2,32,78,4,4]{2,4,1,3,0:T(4,128)(2,1)S(1)} %bitcast.15) | data formatting | bytes 319488 | tf_op jit(solution)/shard_map/transpose | solution.py:377
  2.5 0.3 reshape.7
  2.8 0.2 copy.10
  3.0 0.0 copy-done
  3.0 0.0 copy-done.1
  3.0 0.0 copy-done.2
  3.0 0.0 copy-done.3
  3.0 55.0 %shard_map.68 = (f32[2,32,64]{2,1,0:T(8,128)S(1)}, bf16[32,9984]{1,0:T(8,128)(2,1)S(1)}) custom-call(bf16[32,9984]{1,0:T(8,128)(2,1)S(1)} %copy-done, bf16[512,512]{1,0:T(8,128)(2,1)S(1)} %copy-done.3, bf16[64,1280]{1,0:T(8,128)(2,1)S(1)} %pad.4.x_ref, f32[2,32,64]{2,1,0:T(8,128)S(1)} %bitcast.13, f32[1,64]{1,0:T(1,128)S(1)} %bitcast.14), custom_call_target="tpu_custom_call" | custom-call | flops 1000000000 | bytes 4000000 | tf_op jit(solution)/shard_map/pallas_call | solution.py:384
  58.1 1.1 %convert_multiply_fusion = f32[32,9984]{1,0:T(8,128)} fusion(bf16[32,9984]{1,0:T(8,128)(2,1)S(1)} %get-tuple-element.5), kind=kLoop, calls=%fused_computation | loop fusion | flops 638976 | bytes 1916928 | tf_op jit(solution)/shard_map/mul | solution.py:423
  59.2 0.6 %copy.12 = f32[1,64,2,32]{1,3,2,0:T(8,128)} copy(f32[1,64,2,32]{1,3,2,0:T(8,128)S(1)} %bitcast.12) | data formatting | bytes 32768
  (1 shorter events, 0.0 us)
Async XLA Ops:
  1.8 1.2 %copy-start = (bf16[32,9984]{1,0:T(8,128)(2,1)S(1)}, bf16[32,9984]{1,0:T(8,128)(2,1)}, u32[]{:S(2)}) copy-start(bf16[32,9984]{1,0:T(8,128)(2,1)} %d_ref.1) | copy-start | bytes 1916932
  1.8 1.2 %copy-start.1 = (f32[1,64,2,32]{1,3,2,0:T(8,128)S(1)}, f32[1,64,2,32]{1,3,2,0:T(8,128)}, u32[]{:S(2)}) copy-start(f32[1,64,2,32]{1,3,2,0:T(8,128)} %param.7) | copy-start | bytes 49156
  1.8 1.2 %copy-start.2 = (f32[64]{0:T(128)S(1)}, f32[64]{0:T(128)}, u32[]{:S(2)}) copy-start(f32[64]{0:T(128)} %param.8) | copy-start | bytes 772
  1.8 1.2 %copy-start.3 = (bf16[512,512]{1,0:T(8,128)(2,1)S(1)}, bf16[512,512]{1,0:T(8,128)(2,1)}, u32[]{:S(2)}) copy-start(bf16[512,512]{1,0:T(8,128)(2,1)} %constant.7.clone.p_ref) | copy-start | bytes 1572868
